TPU v7x, 32 devices: a whole 2x2x4 slice. The times are simulated.
32 devices in a mesh: wide: 16 (over z, y, x), narrow: 2 (over core).
Axes of the slice: x: 2, y: 2, z: 4, core: 2. Of those that a mesh axis runs over, the one named last changes fastest.
Arguments:
- tokens: bfloat16 [32768, 768], P(('wide', 'narrow')), may hold values from -6 to 6
- seq_lengths: int32 [32, 4], P(('wide', 'narrow')), may hold values from 0 to 1024, as said below
- w_query: bfloat16 [768, 768], P('wide'), may hold values from -0.21875 to 0.21875
- w_key: bfloat16 [768, 768], P('wide'), may hold values from -0.21875 to 0.21875
- w_value: bfloat16 [768, 768], P('wide'), may hold values from -0.21875 to 0.21875
- w_out: bfloat16 [768, 768], P('wide'), may hold values from -0.625 to 0.625
- w_gate: bfloat16 [768, 2048], P('wide'), may hold values from -0.21875 to 0.21875
- w_up: bfloat16 [768, 2048], P('wide'), may hold values from -0.21875 to 0.21875
- w_down: bfloat16 [2048, 768], P('wide'), may hold values from -0.25 to 0.25
- attn_gain: bfloat16 [768], P('wide'), may hold values from 0.5 to 1.5
- ffn_gain: bfloat16 [768], P('wide'), may hold values from 0.5 to 1.5
- cotangent: bfloat16 [32768, 768], P(('wide', 'narrow')), may hold values from -6 to 6
Outputs:
- output: bfloat16 [32768, 768], P(('wide', 'narrow'))
- grad_tokens: bfloat16 [32768, 768], P(('wide', 'narrow'))
- grad_w_query: float32 [768, 768], P('wide')
- grad_w_key: float32 [768, 768], P('wide')
- grad_w_value: float32 [768, 768], P('wide')
- grad_w_out: float32 [768, 768], P('wide')
- grad_w_gate: float32 [768, 2048], P('wide')
- grad_w_up: float32 [768, 2048], P('wide')
- grad_w_down: float32 [2048, 768], P('wide')
- grad_attn_gain: float32 [768], P('wide')
- grad_ffn_gain: float32 [768], P('wide')
Inputs may be any that keep to these rules, and one draw needn't show every extreme that they name: `seq_lengths`: each row lists the lengths of one device's sequences, each 0, 256, 512 or 1024, summing to 1024, zeros last; some device holds one sequence of 1024.
All inputs are finite; a program needn't handle non-finite values.
Results may differ from a plain program's by a relative error of at most 0.017.
Values may be sent and summed in bfloat16 or wider, within the bound.
A program may use at most 320 MiB of HBM per device.

v0:
```python
import math

import jax
import jax.numpy as jnp
from jax import lax
from jax.sharding import PartitionSpec as P

HEADS = 12


EPS = 1e-06


def layout(lengths, tok_count):
    seq_ends = jnp.cumsum(lengths)
    starts = seq_ends - lengths
    places = jnp.arange(tok_count, dtype=jnp.int32)
    segment = jnp.sum((places[:, None] >= seq_ends[None, :]).astype(jnp.int32), axis=1)
    slot_ids = jnp.arange(lengths.shape[0], dtype=jnp.int32)
    starts_at = jnp.sum(
        jnp.where(segment[:, None] == slot_ids[None, :], starts[None, :], 0), axis=1
    )
    return (segment, places - starts_at)


def rope_tables(positions, head_dim):
    half_dim = head_dim // 2
    column = jnp.arange(half_dim, dtype=jnp.float32)
    frequency = jnp.exp(column * (-2.0 * math.log(10000.0) / head_dim))
    angles = positions.astype(jnp.float32)[:, None] * frequency[None, :]
    angles = jnp.concatenate([angles, angles], axis=1)
    return (jnp.cos(angles), jnp.sin(angles))


def rotate(values, cosine, sine):
    half_dim = values.shape[-1] // 2
    turned = jnp.concatenate([-values[..., half_dim:], values[..., :half_dim]], axis=-1)
    return values * cosine[:, None, :] + turned * sine[:, None, :]


def norm_gain(values, gain):
    return values * lax.rsqrt(jnp.mean(values * values, axis=-1, keepdims=True) + EPS) * gain


def swiglu(gate, upward):
    return jax.nn.silu(gate) * upward


def outer_sum(left, right):
    return lax.dot_general(
        left, right, (((0,), (0,)), ((), ())), preferred_element_type=jnp.float32
    )


def back_dot(rows_in, weight):
    return lax.dot_general(
        rows_in, weight, (((1,), (1,)), ((), ())), preferred_element_type=jnp.float32
    )


def block_scores(query_blk, key_rows, segment, row_index, row_start, scale):
    blk_rows = query_blk.shape[0]
    scores = (
        jnp.einsum("qhd,khd->hqk", query_blk, key_rows, preferred_element_type=jnp.float32) * scale
    )
    seg_blk = segment[row_start : row_start + blk_rows]
    row_blk = row_index[row_start : row_start + blk_rows]
    allowed = (seg_blk[:, None] == segment[None, :]) & (row_index[None, :] <= row_blk[:, None])
    return jnp.where(allowed[None], scores, -1e30)


def attend_forward(queries, key_rows, value_rows, segment):
    tok_count, head_count, head_dim = queries.shape
    scale = head_dim ** (-0.5)
    block_rows = min(512, tok_count)
    row_index = jnp.arange(tok_count, dtype=jnp.int32)
    outputs, totals = ([], [])
    for row_start in range(0, tok_count, block_rows):
        query_blk = queries[row_start : row_start + block_rows]
        scores = block_scores(query_blk, key_rows, segment, row_index, row_start, scale)
        peak = jnp.max(scores, axis=-1, keepdims=True)
        expd = jnp.exp(scores - peak)
        row_mass = jnp.sum(expd, axis=-1, keepdims=True)
        probs_low = (expd / row_mass).astype(jnp.bfloat16)
        outputs.append(
            jnp.einsum("hqk,khd->qhd", probs_low, value_rows, preferred_element_type=jnp.float32)
        )
        totals.append(peak[..., 0] + jnp.log(row_mass[..., 0]))
    return (jnp.concatenate(outputs, axis=0), jnp.concatenate(totals, axis=1))


def attend_backward(queries, key_rows, value_rows, log_total, grad_rows, segment):
    tok_count, head_count, head_dim = queries.shape
    scale = head_dim ** (-0.5)
    block_rows = min(512, tok_count)
    row_index = jnp.arange(tok_count, dtype=jnp.int32)
    grad_keys = jnp.zeros((tok_count, head_count, head_dim), jnp.float32)
    grad_values = jnp.zeros((tok_count, head_count, head_dim), jnp.float32)
    grad_queries = []
    for row_start in range(0, tok_count, block_rows):
        query_blk = queries[row_start : row_start + block_rows]
        grad_blk = grad_rows[row_start : row_start + block_rows]
        scores = block_scores(query_blk, key_rows, segment, row_index, row_start, scale)
        probs = jnp.exp(scores - log_total[:, row_start : row_start + block_rows, None])
        probs_low = probs.astype(jnp.bfloat16)
        grad_probs = jnp.einsum(
            "qhd,khd->hqk", grad_blk, value_rows, preferred_element_type=jnp.float32
        )
        inner = jnp.sum(probs * grad_probs, axis=-1, keepdims=True)
        grad_scores = (probs * (grad_probs - inner)).astype(jnp.bfloat16)
        grad_queries.append(
            jnp.einsum("hqk,khd->qhd", grad_scores, key_rows, preferred_element_type=jnp.float32)
            * scale
        )
        grad_keys = (
            grad_keys
            + jnp.einsum("hqk,qhd->khd", grad_scores, query_blk, preferred_element_type=jnp.float32)
            * scale
        )
        grad_values = grad_values + jnp.einsum(
            "hqk,qhd->khd", probs_low, grad_blk, preferred_element_type=jnp.float32
        )
    return (jnp.concatenate(grad_queries, axis=0), grad_keys, grad_values)


def body(
    tokens,
    seq_lengths,
    w_query,
    w_key,
    w_value,
    w_out,
    w_gate,
    w_up,
    w_down,
    attn_gain,
    ffn_gain,
    cotangent,
):
    gathered = (
        lax.all_gather(w_query, "wide", axis=0, tiled=True),
        lax.all_gather(w_key, "wide", axis=0, tiled=True),
        lax.all_gather(w_value, "wide", axis=0, tiled=True),
        lax.all_gather(w_out, "wide", axis=0, tiled=True),
        lax.all_gather(w_gate, "wide", axis=0, tiled=True),
        lax.all_gather(w_up, "wide", axis=0, tiled=True),
        lax.all_gather(w_down, "wide", axis=0, tiled=True),
        lax.all_gather(attn_gain, "wide", axis=0, tiled=True),
        lax.all_gather(ffn_gain, "wide", axis=0, tiled=True),
    )
    (
        full_query,
        full_key,
        full_value,
        full_out,
        full_gate,
        full_up,
        full_down,
        gain_one,
        gain_two,
    ) = gathered
    gain_one = gain_one.astype(jnp.float32)
    gain_two = gain_two.astype(jnp.float32)
    tok_count, d_model = tokens.shape
    head_count = HEADS
    head_dim = d_model // head_count
    segment, positions = layout(seq_lengths[0], tok_count)
    cosine, sine = rope_tables(positions, head_dim)
    inputs = tokens.astype(jnp.float32)
    h_one = norm_gain(inputs, gain_one).astype(jnp.bfloat16)
    q_pre = jnp.dot(h_one, full_query, preferred_element_type=jnp.float32).reshape(
        tok_count, head_count, head_dim
    )
    k_pre = jnp.dot(h_one, full_key, preferred_element_type=jnp.float32).reshape(
        tok_count, head_count, head_dim
    )
    queries = rotate(q_pre, cosine, sine).astype(jnp.bfloat16)
    key_rows = rotate(k_pre, cosine, sine).astype(jnp.bfloat16)
    value_rows = (
        jnp.dot(h_one, full_value, preferred_element_type=jnp.float32)
        .astype(jnp.bfloat16)
        .reshape(tok_count, head_count, head_dim)
    )
    attended, log_total = attend_forward(queries, key_rows, value_rows, segment)
    attended = attended.reshape(tok_count, d_model).astype(jnp.bfloat16)
    middle = inputs + jnp.dot(attended, full_out, preferred_element_type=jnp.float32)
    h_two = norm_gain(middle, gain_two).astype(jnp.bfloat16)
    gate = jnp.dot(h_two, full_gate, preferred_element_type=jnp.float32)
    upward = jnp.dot(h_two, full_up, preferred_element_type=jnp.float32)
    hidden = swiglu(gate, upward).astype(jnp.bfloat16)
    result = middle + jnp.dot(hidden, full_down, preferred_element_type=jnp.float32)
    output = result.astype(jnp.bfloat16)
    again = (
        lax.all_gather(w_query, "wide", axis=0, tiled=True),
        lax.all_gather(w_key, "wide", axis=0, tiled=True),
        lax.all_gather(w_value, "wide", axis=0, tiled=True),
        lax.all_gather(w_out, "wide", axis=0, tiled=True),
        lax.all_gather(w_gate, "wide", axis=0, tiled=True),
        lax.all_gather(w_up, "wide", axis=0, tiled=True),
        lax.all_gather(w_down, "wide", axis=0, tiled=True),
        lax.all_gather(attn_gain, "wide", axis=0, tiled=True),
        lax.all_gather(ffn_gain, "wide", axis=0, tiled=True),
    )
    (
        full_query,
        full_key,
        full_value,
        full_out,
        full_gate,
        full_up,
        full_down,
        gain_one,
        gain_two,
    ) = again
    gain_one = gain_one.astype(jnp.float32)
    gain_two = gain_two.astype(jnp.float32)
    grad_out_rows = cotangent.astype(jnp.float32)
    grad_down = outer_sum(hidden, cotangent)
    grad_hidden = back_dot(cotangent, full_down)
    mix_value, mix_back = jax.vjp(swiglu, gate, upward)
    grad_gate_f, grad_up_f = mix_back(grad_hidden)
    grad_gate_rows = grad_gate_f.astype(jnp.bfloat16)
    grad_up_rows = grad_up_f.astype(jnp.bfloat16)
    grad_gate = outer_sum(h_two, grad_gate_rows)
    grad_up = outer_sum(h_two, grad_up_rows)
    grad_h_two = back_dot(grad_gate_rows, full_gate) + back_dot(grad_up_rows, full_up)
    norm_value_two, norm_back_two = jax.vjp(norm_gain, middle, gain_two)
    grad_mid_norm, grad_gain_two = norm_back_two(grad_h_two)
    grad_middle = grad_out_rows + grad_mid_norm
    grad_mid_low = grad_middle.astype(jnp.bfloat16)
    grad_out_proj = outer_sum(attended, grad_mid_low)
    grad_attended = (
        back_dot(grad_mid_low, full_out)
        .astype(jnp.bfloat16)
        .reshape(tok_count, head_count, head_dim)
    )
    grad_q, grad_k, grad_v = attend_backward(
        queries, key_rows, value_rows, log_total, grad_attended, segment
    )
    rot_value, rot_back = jax.vjp(lambda turned_in: rotate(turned_in, cosine, sine), q_pre)
    grad_q_pre = rot_back(grad_q)[0].astype(jnp.bfloat16).reshape(tok_count, d_model)
    grad_k_pre = rot_back(grad_k)[0].astype(jnp.bfloat16).reshape(tok_count, d_model)
    grad_v_low = grad_v.astype(jnp.bfloat16).reshape(tok_count, d_model)
    grad_query = outer_sum(h_one, grad_q_pre)
    grad_key = outer_sum(h_one, grad_k_pre)
    grad_value = outer_sum(h_one, grad_v_low)
    grad_h_one = (
        back_dot(grad_q_pre, full_query)
        + back_dot(grad_k_pre, full_key)
        + back_dot(grad_v_low, full_value)
    )
    norm_value_one, norm_back_one = jax.vjp(norm_gain, inputs, gain_one)
    grad_in_norm, grad_gain_one = norm_back_one(grad_h_one)
    grad_tokens = (grad_middle + grad_in_norm).astype(jnp.bfloat16)
    wide_shares = (
        lax.psum_scatter(grad_query, "wide", scatter_dimension=0, tiled=True),
        lax.psum_scatter(grad_key, "wide", scatter_dimension=0, tiled=True),
        lax.psum_scatter(grad_value, "wide", scatter_dimension=0, tiled=True),
        lax.psum_scatter(grad_out_proj, "wide", scatter_dimension=0, tiled=True),
        lax.psum_scatter(grad_gate, "wide", scatter_dimension=0, tiled=True),
        lax.psum_scatter(grad_up, "wide", scatter_dimension=0, tiled=True),
        lax.psum_scatter(grad_down, "wide", scatter_dimension=0, tiled=True),
        lax.psum_scatter(grad_gain_one, "wide", scatter_dimension=0, tiled=True),
        lax.psum_scatter(grad_gain_two, "wide", scatter_dimension=0, tiled=True),
    )
    summed = (
        lax.psum(wide_shares[0].astype(jnp.bfloat16), "narrow").astype(jnp.float32),
        lax.psum(wide_shares[1].astype(jnp.bfloat16), "narrow").astype(jnp.float32),
        lax.psum(wide_shares[2].astype(jnp.bfloat16), "narrow").astype(jnp.float32),
        lax.psum(wide_shares[3].astype(jnp.bfloat16), "narrow").astype(jnp.float32),
        lax.psum(wide_shares[4].astype(jnp.bfloat16), "narrow").astype(jnp.float32),
        lax.psum(wide_shares[5].astype(jnp.bfloat16), "narrow").astype(jnp.float32),
        lax.psum(wide_shares[6].astype(jnp.bfloat16), "narrow").astype(jnp.float32),
        lax.psum(wide_shares[7].astype(jnp.bfloat16), "narrow").astype(jnp.float32),
        lax.psum(wide_shares[8].astype(jnp.bfloat16), "narrow").astype(jnp.float32),
    )
    return (
        output,
        grad_tokens,
        summed[0],
        summed[1],
        summed[2],
        summed[3],
        summed[4],
        summed[5],
        summed[6],
        summed[7],
        summed[8],
    )


def solution(mesh):
    in_specs = (
        P(("wide", "narrow"), None),
        P(("wide", "narrow"), None),
        P("wide", None),
        P("wide", None),
        P("wide", None),
        P("wide", None),
        P("wide", None),
        P("wide", None),
        P("wide", None),
        P("wide"),
        P("wide"),
        P(("wide", "narrow"), None),
    )
    out_specs = (
        P(("wide", "narrow"), None),
        P(("wide", "narrow"), None),
        P("wide", None),
        P("wide", None),
        P("wide", None),
        P("wide", None),
        P("wide", None),
        P("wide", None),
        P("wide", None),
        P("wide"),
        P("wide"),
    )
    return jax.shard_map(body, mesh=mesh, in_specs=in_specs, out_specs=out_specs, check_vma=False)
```

profile of v0, /device:TPU:0, one launch (start us, length us, event | category | flops | bytes accessed | tf_op | source)
XLA Modules:
  0.0 1542.8 jit_solution(829165757414737824)
XLA Ops:
  17.1 43.8 %all-reduce.9 = (bf16[768]{0:T(1024)(128)(2,1)S(1)}, bf16[768]{0:T(1024)(128)(2,1)S(1)}) all-reduce(bf16[768]{0:T(1024)(128)(2,1)S(1)} %dynamic-update-slice, bf16[768]{0:T(1024)(128)(2,1)S(1)} %dynamic-update-slice.1), channel_id=1, replica_groups=mesh['wide'=16,'narrow'=2] {'wide'}, use_global_device_ids=true, to_apply=%add.4 | all-reduce | flops 1536 | bytes 6144
  76.6 51.0 %all-gather.10.cloned.1.call-done = bf16[768,768]{1,0:T(8,128)(2,1)} async-done(((bf16[48,768]{1,0:T(8,128)(2,1)}), bf16[768,768]{1,0:T(8,128)(2,1)}) %all-gather.10.cloned.1.call-update) | async-done | bytes 1179664 | tf_op jit(solution)/shard_map/all_gather | solution.py:141
  135.1 10.7 fusion.13
  145.8 10.7 fusion.12
  156.5 12.0 fusion.1
  168.5 17.0 %all-gather.8.cloned.1.call-done = bf16[768,768]{1,0:T(8,128)(2,1)} async-done(((bf16[48,768]{1,0:T(8,128)(2,1)}), bf16[768,768]{1,0:T(8,128)(2,1)}) %all-gather.8.cloned.1.call-update) | async-done | bytes 1179664 | tf_op jit(solution)/shard_map/all_gather | solution.py:143
  188.3 14.3 fusion.42
  211.9 8.9 fusion.41
  223.5 19.7 %all-gather.14.cloned.1.call-done = bf16[768,768]{1,0:T(8,128)(2,1)} async-done(((bf16[48,768]{1,0:T(8,128)(2,1)}), bf16[768,768]{1,0:T(8,128)(2,1)}) %all-gather.14.cloned.1.call-update) | async-done | bytes 1179664 | tf_op jit(solution)/shard_map/all_gather | solution.py:144
  249.8 63.1 %all-gather.18.cloned.1.call-done = bf16[768,2048]{1,0:T(8,128)(2,1)} async-done(((bf16[48,2048]{1,0:T(8,128)(2,1)}), bf16[768,2048]{1,0:T(8,128)(2,1)}) %all-gather.18.cloned.1.call-update) | async-done | bytes 3145744 | tf_op jit(solution)/shard_map/all_gather | solution.py:146
  312.8 9.1 fusion.83
  321.9 60.2 %all-gather.16.cloned.1.call-done = bf16[768,2048]{1,0:T(8,128)(2,1)} async-done(((bf16[48,2048]{1,0:T(8,128)(2,1)}), bf16[768,2048]{1,0:T(8,128)(2,1)}) %all-gather.16.cloned.1.call-update) | async-done | bytes 3145744 | tf_op jit(solution)/shard_map/all_gather | solution.py:145
  382.1 9.1 fusion.82
  391.2 60.3 %all-gather.20.cloned.1.call-done = bf16[2048,768]{1,0:T(8,128)(2,1)} async-done(((bf16[128,768]{1,0:T(8,128)(2,1)}), bf16[2048,768]{1,0:T(8,128)(2,1)}) %all-gather.20.cloned.1.call-update) | async-done | bytes 3145744 | tf_op jit(solution)/shard_map/all_gather | solution.py:147
  451.6 14.4 multiply_convert_fusion.2
  488.0 12.0 fusion.4
  500.1 12.0 add_convert_fusion
  516.1 18.3 %multiply_reduce_fusion.1 = (f32[12,512]{1,0:T(8,128)S(1)}, f32[12,512,1024]{2,1,0:T(8,128)}) fusion(f32[12,512]{1,0:T(8,128)S(1)} %log_add_fusion.1, f32[12,512,1024]{2,1,0:T(8,128)} %get-tuple-element.89, pred[512,1024]{1,0:T(8,128)(4,1)S(1)} %get-tuple-element.80, bf16[512,12,64]{0,2,1:T(8,128)(2,1)} %bitcast.100, bf16[1024,12,64]{0,2,1:T(8,128)(2,1)} %bitcast.96), kind=kOutput, calls=%fused_computation.4 | convolution fusion | flops 836757504 | bytes 53264384 | tf_op jit(solution)/shard_map/qhd,khd->hqk/dot_general | solution.py:106
  534.3 18.7 %multiply_reduce_fusion = (f32[12,512]{1,0:T(8,128)S(1)}, f32[12,512,1024]{2,1,0:T(8,128)}) fusion(f32[12,512]{1,0:T(8,128)S(1)} %log_add_fusion, f32[12,512,1024]{2,1,0:T(8,128)} %get-tuple-element.87, pred[512,1024]{1,0:T(8,128)(4,1)S(1)} %get-tuple-element.81, bf16[512,12,64]{0,2,1:T(8,128)(2,1)} %bitcast.99, bf16[1024,12,64]{0,2,1:T(8,128)(2,1)} %bitcast.97), kind=kOutput, calls=%fused_computation.1 | convolution fusion | flops 836757504 | bytes 53264384 | tf_op jit(solution)/shard_map/qhd,khd->hqk/dot_general | solution.py:106
  553.1 42.2 %multiply_convert_fusion = (bf16[12,512,1024]{2,1,0:T(8,128)(2,1)}, bf16[12,512,1024]{2,1,0:T(8,128)(2,1)}) fusion(f32[12,512,1024]{2,1,0:T(8,128)} %get-tuple-element.94, f32[12,512]{1,0:T(8,128)S(1)} %get-tuple-element.93, f32[12,512]{1,0:T(8,128)S(1)} %log_add_fusion, f32[12,512,1024]{2,1,0:T(8,128)} %get-tuple-element.87, ...), kind=kLoop, calls=%fused_computation | loop fusion | flops 75497472 | bytes 126976000 | tf_op jit(solution)/shard_map/convert_element_type | solution.py:110
  613.4 8.5 multiply_bitcast_fusion
  621.9 8.5 multiply_bitcast_fusion.1
  636.8 7.5 fusion.86
  644.4 7.6 fusion.85
  653.4 8.3 fusion.87
  676.7 71.7 %reduce-scatter.12.cloned.1.call-done = f32[48,768]{1,0:T(8,128)} async-done(((f32[768,768]{1,0:T(8,128)}), f32[48,768]{1,0:T(8,128)}) %reduce-scatter.12.cloned.1.call-update) | async-done | bytes 147472 | tf_op jit(solution)/shard_map/reduce_scatter | solution.py:258
  750.0 130.9 %reduce-scatter.10.cloned.1.call-done = f32[48,768]{1,0:T(8,128)} async-done(((f32[768,768]{1,0:T(8,128)}), f32[48,768]{1,0:T(8,128)}) %reduce-scatter.10.cloned.1.call-update) | async-done | bytes 147472 | tf_op jit(solution)/shard_map/reduce_scatter | solution.py:257
  882.4 131.8 %reduce-scatter.8.cloned.1.call-done = f32[48,768]{1,0:T(8,128)} async-done(((f32[768,768]{1,0:T(8,128)}), f32[48,768]{1,0:T(8,128)}) %reduce-scatter.8.cloned.1.call-update) | async-done | bytes 147472 | tf_op jit(solution)/shard_map/reduce_scatter | solution.py:256
  1015.7 148.3 %reduce-scatter.18.cloned.1.call-done = f32[48,2048]{1,0:T(8,128)} async-done(((f32[768,2048]{1,0:T(8,128)}), f32[48,2048]{1,0:T(8,128)}) %reduce-scatter.18.cloned.1.call-update) | async-done | bytes 393232 | tf_op jit(solution)/shard_map/reduce_scatter | solution.py:261
  1165.7 148.8 %reduce-scatter.16.cloned.1.call-done = f32[48,2048]{1,0:T(8,128)} async-done(((f32[768,2048]{1,0:T(8,128)}), f32[48,2048]{1,0:T(8,128)}) %reduce-scatter.16.cloned.1.call-update) | async-done | bytes 393232 | tf_op jit(solution)/shard_map/reduce_scatter | solution.py:260
  1316.2 148.6 %reduce-scatter.20.cloned.1.call-done = f32[128,768]{1,0:T(8,128)} async-done(((f32[2048,768]{1,0:T(8,128)}), f32[128,768]{1,0:T(8,128)}) %reduce-scatter.20.cloned.1.call-update) | async-done | bytes 393232 | tf_op jit(solution)/shard_map/reduce_scatter | solution.py:262
  1475.3 40.4 %all-reduce.8 = (bf16[768]{0:T(1024)(128)(2,1)S(1)}, bf16[768]{0:T(1024)(128)(2,1)S(1)}) all-reduce(f32[768]{0:T(1024)S(1)} %get-tuple-element.46, f32[768]{0:T(1024)S(1)} %copy-done.37), channel_id=9, replica_groups=mesh['wide'=16,'narrow'=2] {'wide'}, use_global_device_ids=true, to_apply=%region_28.29.clone | all-reduce | flops 1536 | bytes 9216
  (216 shorter events, 158.1 us)
Async XLA Ops:
  7.2 63.1 %all-gather.12.cloned.1.call-start = ((), (), s32[]{:S(2)}) async-start(), calls=%async_computation.9 | async-start | bytes 1253376 | tf_op jit(solution)/shard_map/all_gather | solution.py:142
  7.9 119.7 %all-gather.10.cloned.1.call-start = ((), (), s32[]{:S(2)}) async-start(), calls=%async_computation.8 | async-start | bytes 1253376 | tf_op jit(solution)/shard_map/all_gather | solution.py:141
  8.7 176.8 %all-gather.8.cloned.1.call-start = ((), (), s32[]{:S(2)}) async-start(), calls=%async_computation.7 | async-start | bytes 1253376 | tf_op jit(solution)/shard_map/all_gather | solution.py:143
  9.4 233.8 %all-gather.14.cloned.1.call-start = ((), (), s32[]{:S(2)}) async-start(), calls=%async_computation.10 | async-start | bytes 1253376 | tf_op jit(solution)/shard_map/all_gather | solution.py:144
  10.0 302.9 %all-gather.18.cloned.1.call-start = ((), (), s32[]{:S(2)}) async-start(), calls=%async_computation.12 | async-start | bytes 3342336 | tf_op jit(solution)/shard_map/all_gather | solution.py:146
  10.6 371.6 %all-gather.16.cloned.1.call-start = ((), (), s32[]{:S(2)}) async-start(), calls=%async_computation.11 | async-start | bytes 3342336 | tf_op jit(solution)/shard_map/all_gather | solution.py:145
  11.1 440.4 %all-gather.20.cloned.1.call-start = ((), (), s32[]{:S(2)}) async-start(), calls=%async_computation.13 | async-start | bytes 3342336 | tf_op jit(solution)/shard_map/all_gather | solution.py:147
  11.9 663.2 %reduce-scatter.14.cloned.1.call-start = ((), (), s32[]{:S(2)}) async-start(), calls=%async_computation.17 | async-start | bytes 2506752 | tf_op jit(solution)/shard_map/reduce_scatter | solution.py:259
  60.9 124.5 %copy-start.30 = (f32[768]{0:T(1024)}, f32[768]{0:T(1024)S(1)}, u32[]{:S(2)}) copy-start(f32[768]{0:T(1024)S(1)} %convert_element_type.149) | copy-start | bytes 9220
  63.6 67.3 %copy-start.17 = (f32[1024,64]{0,1:T(8,128)}, f32[1024,64]{0,1:T(8,128)S(1)}, u32[]{:S(2)}) copy-start(f32[1024,64]{0,1:T(8,128)S(1)} %get-tuple-element.79) | copy-start | bytes 786436
  63.6 67.4 %copy-start.19 = (f32[1024,64]{0,1:T(8,128)}, f32[1024,64]{0,1:T(8,128)S(1)}, u32[]{:S(2)}) copy-start(f32[1024,64]{0,1:T(8,128)S(1)} %get-tuple-element.78) | copy-start | bytes 786436
  66.4 119.0 %copy-start.32 = (f32[1024]{0:T(1024)}, f32[1024]{0:T(1024)S(1)}, u32[]{:S(2)}) copy-start(f32[1024]{0:T(1024)S(1)} %fusion.55) | copy-start | bytes 12292
  188.2 23.7 %copy-start.11 = (bf16[1024,768]{0,1:T(8,128)(2,1)}, bf16[1024,768]{0,1:T(8,128)(2,1)S(1)}, u32[]{:S(2)}) copy-start(bf16[1024,768]{0,1:T(8,128)(2,1)S(1)} %convolution_convert_fusion.1) | copy-start | bytes 4718596
  188.2 14.3 slice-start
  188.2 14.3 slice-start.1
  188.3 14.3 slice-start.2
  188.3 14.3 slice-start.3
  188.3 15.1 slice-start.4
  188.3 16.3 %slice-start.5 = ((s8[25165824]{0:T(1024)(128)(4,1)}), s8[4194304]{0:T(1024)(128)(4,1)S(1)}, s32[]{:S(2)}) async-start(s8[25165824]{0:T(1024)(128)(4,1)} %bitcast.88), calls=%async_computation.27 | async-start | bytes 8388608
  451.6 14.4 copy-start.40
  487.9 260.5 %reduce-scatter.12.cloned.1.call-start = ((), (), s32[]{:S(2)}) async-start(), calls=%async_computation.16 | async-start | bytes 2506752 | tf_op jit(solution)/shard_map/reduce_scatter | solution.py:258
  488.0 12.1 copy-start.15
  500.1 13.1 copy-start.31
  500.1 13.1 copy-start.33
  553.1 327.8 %reduce-scatter.10.cloned.1.call-start = ((), (), s32[]{:S(2)}) async-start(), calls=%async_computation.15 | async-start | bytes 2506752 | tf_op jit(solution)/shard_map/reduce_scatter | solution.py:257
  553.1 42.2 %copy-start.4 = (bf16[1024,12,64]{0,2,1:T(8,128)(2,1)S(1)}, bf16[1024,12,64]{0,2,1:T(8,128)(2,1)}, u32[]{:S(2)}) copy-start(bf16[1024,12,64]{0,2,1:T(8,128)(2,1)} %copy-done.3) | copy-start | bytes 4718596
  612.0 402.2 %reduce-scatter.8.cloned.1.call-start = ((), (), s32[]{:S(2)}) async-start(), calls=%async_computation.14 | async-start | bytes 2506752 | tf_op jit(solution)/shard_map/reduce_scatter | solution.py:256
  636.7 527.3 %reduce-scatter.18.cloned.1.call-start = ((), (), s32[]{:S(2)}) async-start(), calls=%async_computation.19 | async-start | bytes 6684672 | tf_op jit(solution)/shard_map/reduce_scatter | solution.py:261
  644.3 670.2 %reduce-scatter.16.cloned.1.call-start = ((), (), s32[]{:S(2)}) async-start(), calls=%async_computation.18 | async-start | bytes 6684672 | tf_op jit(solution)/shard_map/reduce_scatter | solution.py:260
  652.0 812.9 %reduce-scatter.20.cloned.1.call-start = ((), (), s32[]{:S(2)}) async-start(), calls=%async_computation.20 | async-start | bytes 6684672 | tf_op jit(solution)/shard_map/reduce_scatter | solution.py:262
  661.7 862.8 %all-reduce.14.cloned.1.call-start = ((), (), s32[]{:S(2)}) async-start(), calls=%async_computation.21 | async-start | bytes 1769472 | tf_op jit(solution)/shard_map/psum | solution.py:267
  1473.7 42.1 %copy-start.36 = (f32[1024]{0:T(1024)S(1)}, f32[1024]{0:T(1024)}, u32[]{:S(2)}) copy-start(f32[1024]{0:T(1024)} %copy-done.35) | copy-start | bytes 12292
  (33 other events, 130.4 us)
Sparse Core Ops, SparseCore 0:
  10.8 58.9 all-gather.11
  72.6 54.9 all-gather.9
  130.4 54.9 all-gather.7
  188.1 55.0 all-gather.13
  245.8 67.0 all-gather.17
  315.5 66.6 all-gather.15
  384.9 66.6 all-gather.19
  488.1 126.9 reduce-scatter.13
  620.8 127.5 reduce-scatter.11
  753.2 127.6 reduce-scatter.9
  886.5 127.5 reduce-scatter.7
  1019.3 144.7 reduce-scatter.17
  1169.3 145.2 reduce-scatter.15
  1319.6 145.1 reduce-scatter.19
  1468.7 18.9 all-reduce.13
where the time goes:
time: 1550 us; the launch traced here: 1540 us
  waiting for transfers between devices  1060 us (68%)
  matrix products  245 us (16%)
  other arithmetic  107 us (7%)
  blocking collectives  86.7 us (6%)
  local copies, waits for them, and re-layouts  31.6 us (2%)
  between operations  16.4 us (1%)
    reduce_scatter x1, waiting for transfers between devices, body(): lax.psum_scatter(grad_gate, 'wide', scatter_dimension=0, tiled=True)  149 us
    reduce_scatter x1, waiting for transfers between devices, body(): lax.psum_scatter(grad_down, 'wide', scatter_dimension=0, tiled=True)  149 us
    reduce_scatter x1, waiting for transfers between devices, body(): lax.psum_scatter(grad_up, 'wide', scatter_dimension=0, tiled=True)  148 us
    reduce_scatter x1, waiting for transfers between devices, body(): lax.psum_scatter(grad_query, 'wide', scatter_dimension=0, tiled=True)  132 us
    reduce_scatter x1, waiting for transfers between devices, body(): lax.psum_scatter(grad_key, 'wide', scatter_dimension=0, tiled=True)  131 us
    unnamed x2, blocking collectives  84.2 us
    reduce_scatter x1, waiting for transfers between devices, body(): lax.psum_scatter(grad_value, 'wide', scatter_dimension=0, tiled=True)  71.7 us
    all_gather x1, waiting for transfers between devices, body(): lax.all_gather(w_up, 'wide', axis=0, tiled=True)  63.1 us
  transfers between devices with their start and end apart: 15, of which 12 were waited for; matrix products, arithmetic and copies ran while one was open for 20% of the time, Pallas kernels for 0%

commit v1 on v0

--- a/solution.py
+++ b/solution.py
@@ -1,18 +1,864 @@
+import functools
 import math
 
 import jax
 import jax.numpy as jnp
 from jax import lax
+from jax.experimental import pallas as pl
+from jax.experimental.pallas import tpu as pltpu
 from jax.sharding import PartitionSpec as P
 
 HEADS = 12
-
-
 EPS = 1e-06
+NEG = -1e30
+BF = jnp.bfloat16
+F32 = jnp.float32
+MESH = pl.DeviceIdType.MESH
+VMEM_BYTES = 60 * 2**20
+
+
+def nn(left, right):
+    return jnp.dot(left, right, preferred_element_type=F32)
+
+
+def nt(left, right):
+    return lax.dot_general(left, right, (((1,), (1,)), ((), ())), preferred_element_type=F32)
+
+
+def flat(values):
+    return values.reshape(-1, values.shape[-1])
+
+
+def sigmoid(v):
+    return 1.0 / (1.0 + jnp.exp(-v))
+
+
+def three_way(v):
+    high = v.astype(BF)
+    rest = v - high.astype(F32)
+    mid = rest.astype(BF)
+    return high, mid, (rest - mid.astype(F32)).astype(BF)
+
+
+class Place:
+    def __init__(self):
+        wide = lax.axis_index("wide")
+        self.c = lax.axis_index("narrow")
+        self.w = wide
+        self.z = wide // 4
+        self.p = lax.rem(wide, 4)
+        across_y = lax.rem(self.p + 2, 4)
+        across_x = self.p + 1 - 2 * lax.rem(self.p, 2)
+        self.q1 = (1 - self.c) * across_y + self.c * across_x
+        self.q2 = (1 - self.c) * across_x + self.c * across_y
+        self.q3 = 3 - self.p
+        self.first = {"wide": self.z * 4 + self.q1}
+        self.second = {"wide": self.z * 4 + self.q2}
+        self.other = {"narrow": 1 - self.c}
+
+    def z_at(self, d):
+        return lax.rem(self.z + d + 4, 4)
+
+    def z_dev(self, d):
+        return {"wide": self.z_at(d) * 4 + self.p}
+
+
+def enter(place):
+    sem = pltpu.get_barrier_semaphore()
+    for d in range(1, 16):
+        pl.semaphore_signal(sem, inc=1, device_id={"wide": lax.rem(place.w + d, 16)}, device_id_type=MESH)
+    pl.semaphore_signal(sem, inc=1, device_id=place.other, device_id_type=MESH)
+    pl.semaphore_wait(sem, 16)
+
+
+def remote(src, dst, send, recv, device):
+    return pltpu.make_async_remote_copy(
+        src_ref=src, dst_ref=dst, send_sem=send, recv_sem=recv, device_id=device, device_id_type=MESH
+    )
+
+
+def lane_of(rows, lanes=128):
+    return lax.broadcasted_iota(jnp.int32, (rows, lanes), 1)
+
+
+def spread(index):
+    row = lax.broadcasted_iota(jnp.int32, (128, 768), 0)
+    col = lax.broadcasted_iota(jnp.int32, (128, 768), 1)
+    return jnp.where((col == row + 48 * index) & (row < 48), 1.0, 0.0).astype(BF)
+
+
+class Gather:
+    def __init__(self, place, buf, start, width, rows, send, recv):
+        self.place = place
+        r0, rn = rows
+
+        def part(z, q, core):
+            col = pl.ds(pl.multiple_of(start + core * width, 128), width)
+            return buf.at[z, q, pl.ds(r0, rn), col]
+
+        def block(q, core):
+            col = pl.ds(pl.multiple_of(start + core * width, 128), width)
+            return buf.at[:, q, pl.ds(r0, rn), col]
+
+        self.part, self.block, self.send, self.recv = part, block, send, recv
+
+    def copy(self, k, ref, device):
+        return remote(ref, ref, self.send.at[k], self.recv.at[k], device)
+
+
+def block_steps(unit):
+    pc = unit.place
+    me = pc.c
+    zs = [unit.copy(d - 1, unit.part(pc.z, pc.p, me), pc.z_dev(d)) for d in (1, 2, 3)]
+    own = unit.block(pc.p, me)
+    to_first = unit.copy(3, own, pc.first)
+    to_second = unit.copy(4, own, pc.second)
+    on_second = unit.copy(5, unit.block(pc.q1, me), pc.second)
+    cores = [unit.copy(6 + i, unit.block(q, me), pc.other) for i, q in enumerate((pc.p, pc.q1, pc.q2, pc.q3))]
+
+    def s0():
+        for copy in zs:
+            copy.start()
+
+    def s1():
+        for copy in zs:
+            copy.wait_recv()
+        to_first.start()
+        to_second.start()
+        cores[0].start()
+
+    def s2():
+        to_first.wait_recv()
+        on_second.start()
+        cores[1].start()
+
+    def s3():
+        to_second.wait_recv()
+        cores[2].start()
+
+    def s4():
+        on_second.wait_recv()
+        cores[3].start()
+
+    def s5():
+        for copy in cores:
+            copy.wait_recv()
+        for copy in [*zs, to_first, to_second, on_second, *cores]:
+            copy.wait_send()
+
+    return [s0, s1, s2, s3, s4, s5]
+
+
+def piece_gather(unit):
+    pc = unit.place
+    me = pc.c
+    planes = (pc.p, pc.q1, pc.q2, pc.q3)
+    zs = [unit.copy(d - 1, unit.part(pc.z, pc.p, me), pc.z_dev(d)) for d in (1, 2, 3)]
+    first = [unit.copy(3 + d, unit.part(pc.z_at(-d), pc.p, me), pc.first) for d in range(4)]
+    second = [unit.copy(7 + d, unit.part(pc.z_at(-d), pc.p, me), pc.second) for d in range(4)]
+    onward = [unit.copy(11 + d, unit.part(pc.z_at(-d), pc.q1, me), pc.second) for d in range(4)]
+    cores = [[unit.copy(15 + 4 * i + d, unit.part(pc.z_at(-d), q, me), pc.other) for d in range(4)] for i, q in enumerate(planes)]
+    for copy in zs:
+        copy.start()
+    first[0].start()
+    second[0].start()
+    cores[0][0].start()
+    order = (0, 1, 3, 2)
+    for n, d in enumerate(order):
+        if n:
+            zs[d - 1].wait_recv()
+            first[d].start()
+            second[d].start()
+            cores[0][d].start()
+        if n:
+            before = order[n - 1]
+            first[before].wait_recv()
+            onward[before].start()
+            cores[1][before].start()
+            second[before].wait_recv()
+            cores[2][before].start()
+    last = order[-1]
+    first[last].wait_recv()
+    onward[last].start()
+    cores[1][last].start()
+    second[last].wait_recv()
+    cores[2][last].start()
+    for d in order:
+        onward[d].wait_recv()
+        cores[3][d].start()
+    for line in cores:
+        for copy in line:
+            copy.wait_recv()
+    for copy in [*zs, *first, *second, *onward, *sum(cores, [])]:
+        copy.wait_send()
+
+
+def pair_at(j):
+    return lax.rem(j, 2) * 1152 + (j // 2) * 384
+
+
+def fold(units):
+    depth = len(units[0])
+    slots = []
+    for n in range(len(units) + depth - 1):
+        steps = []
+        if n < len(units):
+            steps.append(units[n][0])
+        for s in range(depth - 1, 0, -1):
+            if 0 <= n - s < len(units):
+                steps.append(units[n - s][s])
+        slots.append(steps)
+    return slots
+
+
+def run_all(steps):
+    for step in steps:
+        step()
+
+
+def turned(values, lane, back):
+    up = pltpu.roll(values, 96, 1)
+    down = pltpu.roll(values, 32, 1)
+    low = lax.rem(lane, 64) < 32
+    return jnp.where(low, up, -down) if back else jnp.where(low, -up, down)
+
+
+def fore_kernel(
+    lens, x_ref, dy_ref, gt_hbm, wq, wk, wv, wo, wg, wu, wd,
+    q_out, k_out, v_out, o_out, do_out, h1t_out, lse_out, seg_out, rope_out, w_out, dx2_out, gain_out, gg_out, y_out, gu_sum, d_sum, o_sum,
+    w_s, wo_s, wgu_s, wd_s, gain_s, gains, x2_s, y_s, dh2_s, h1t_s, q_s, k_s, v_s, o_s, lse_s, seg_s, rope_s,
+    hidt_s, dgu_s, gg_s, yb_s, gu_st, d_st, o_st, gu_r, d_r, o_r,
+    wsend, wrecv, usend, urecv, gsend, grecv, rsend, rrecv, lsem, osem,
+):
+    pc = Place()
+    tok = x_ref.shape[0]
+    blocks = tok // 256
+    loads = []
+
+    def load(src, dst):
+        copy = pltpu.make_async_copy(src, dst, lsem.at[len(loads)])
+        copy.start()
+        loads.append(copy)
+
+    def half(start, width):
+        return pl.ds(pl.multiple_of(start + pc.c * width, 128), width)
+
+    load(gt_hbm, gain_s.at[pc.w])
+    for m in range(3):
+        for n, w in enumerate((wq, wk, wv)):
+            load(w.at[:, half(m * 256, 128)], w_s.at[pc.z, pc.p, :, pl.ds(pl.multiple_of(pc.c * 1152 + m * 384 + n * 128, 128), 128)])
+    early = len(loads)
+    load(wo.at[:, half(0, 384)], wo_s.at[pc.z, pc.p, :, half(0, 384)])
+    load(wd.at[:, half(0, 384)], wd_s.at[pc.z, pc.p, :, half(0, 384)])
+    for u in range(4):
+        for n, w in enumerate((wg, wu)):
+            load(w.at[:, half(u * 512, 256)], wgu_s.at[pc.z, pc.p, :, pl.ds(pl.multiple_of(u * 1024 + n * 256 + pc.c * 512, 128), 256)])
+    enter(pc)
+    for copy in loads[:early]:
+        copy.wait()
+    gain_copies = [
+        remote(gain_s.at[pc.w], gain_s.at[pc.w], gsend.at[d - 1], grecv.at[d - 1], {"wide": lax.rem(pc.w + d, 16)}) for d in range(1, 16)
+    ]
+    for copy in gain_copies:
+        copy.start()
+    for copy in loads[early:]:
+        copy.wait()
+    ends, total = [], jnp.int32(0)
+    for s in range(4):
+        total = total + lens[0, s]
+        ends.append(total)
+
+    def tables(r, carry):
+        rs = pl.ds(pl.multiple_of(r * 256, 256), 256)
+        lane = lane_of(256)
+        place = lax.broadcasted_iota(jnp.int32, (256, 128), 0) + r * 256
+        seg = jnp.zeros((256, 128), jnp.int32)
+        start = jnp.zeros((256, 128), jnp.int32)
+        for s in range(4):
+            past = place >= ends[s]
+            seg = seg + past.astype(jnp.int32)
+            start = jnp.where(past, ends[s], start)
+        column = lax.rem(lane, 32).astype(F32)
+        angle = (place - start).astype(F32) * jnp.exp(column * (-2.0 * math.log(10000.0) / 64))
+        rope_s[0, rs, :] = jnp.cos(angle)
+        rope_s[1, rs, :] = jnp.sin(angle)
+        seg_s[0, rs, :] = jnp.where((lane == seg) | (lane >= 4), 0.0, NEG).astype(BF)
+        seg_s[1, rs, :] = jnp.where((lane == seg) | ((lane >= 4) & (lane < 7)), 1.0, 0.0).astype(BF)
+        return carry
+
+    unit_qkv = Gather(pc, w_s, 0, 1152, (0, 48), wsend, wrecv)
+    lax.fori_loop(0, blocks, tables, 0)
+    piece_gather(unit_qkv)
+    for copy in gain_copies:
+        copy.wait_recv()
+
+    def gain_rows(w, rows):
+        return rows + nn(gain_s[w], spread(w))
+
+    gains[...] = lax.fori_loop(0, 16, gain_rows, jnp.zeros((16, 768), F32))
+    units = [
+        Gather(pc, wo_s, 0, 384, (0, 48), usend.at[0], urecv.at[0]),
+        Gather(pc, wd_s, 0, 384, (0, 64), usend.at[1], urecv.at[1]),
+        Gather(pc, wd_s, 0, 384, (64, 64), usend.at[2], urecv.at[2]),
+    ] + [Gather(pc, wgu_s, 1024 * u, 512, (0, 48), usend.at[3 + u], urecv.at[3 + u]) for u in range(4)]
+    slots = fold([block_steps(u) for u in units])
+    outs = []
+
+    def store(src, dst):
+        copy = pltpu.make_async_copy(src, dst, osem.at[len(outs)])
+        copy.start()
+        outs.append(copy)
+        return copy
+
+    run_all(slots[0])
+    store(gains, gain_out)
+    w_copy = store(w_s, w_out)
+    store(seg_s, seg_out)
+    store(rope_s, rope_out)
+
+    def project(r, carry):
+        rs = pl.ds(pl.multiple_of(r * 256, 256), 256)
+        lane = lane_of(256)
+        x = x_ref[rs, :].astype(F32)
+        h1 = (x * lax.rsqrt(jnp.mean(x * x, axis=1, keepdims=True) + EPS) * gains[0:1, :]).astype(BF)
+        h1t_s[:, rs] = h1.T
+        cos, sin = rope_s[0, rs, :], rope_s[1, rs, :]
+        for half in range(2):
+            pre = nn(h1, flat(w_s[:, :, :, half * 1152 : (half + 1) * 1152]))
+            for m in range(3):
+                cs = pl.ds((2 * m + half) * 128, 128)
+                qp, kp, vp = (pre[:, m * 384 + n * 128 : m * 384 + (n + 1) * 128] for n in range(3))
+                q_s[rs, cs] = ((qp * cos + turned(qp, lane, False) * sin).astype(BF).astype(F32) * 0.125).astype(BF)
+                k_s[rs, cs] = (kp * cos + turned(kp, lane, False) * sin).astype(BF)
+                v_s[rs, cs] = vp.astype(BF)
+        return carry
+
+    lax.fori_loop(0, blocks, project, 0)
+    kept = [store(q_s, q_out), store(k_s, k_out), store(v_s, v_out), store(h1t_s, h1t_out)]
+    run_all(slots[1])
+
+    def pair(j, carry):
+        for t in range(6):
+            pl.when(j == t)(functools.partial(run_all, slots[2 + t]))
+        cs = pl.ds(pl.multiple_of(j * 128, 128), 128)
+        lane = lane_of(256)
+        below = lax.broadcasted_iota(jnp.int32, (256, 256), 0) >= lax.broadcasted_iota(jnp.int32, (256, 256), 1)
+        for i in range(blocks):
+            rs, before = pl.ds(i * 256, 256), pl.ds(0, i * 256)
+            qt = q_s[rs, cs]
+            parts = []
+            for h in range(2):
+                qm = jnp.where((lane < 64) == (h == 0), qt, BF(0))
+                qm = jnp.concatenate([qm, seg_s[0, rs, :]], axis=1)
+                sd = jnp.where(below, nt(qm, jnp.concatenate([k_s[rs, cs], seg_s[1, rs, :]], axis=1)), NEG)
+                top = jnp.max(sd, axis=1, keepdims=True)
+                if i:
+                    so = nt(qm, jnp.concatenate([k_s[before, cs], seg_s[1, before, :]], axis=1))
+                    top = jnp.maximum(top, jnp.max(so, axis=1, keepdims=True))
+                pd = jnp.exp(sd - top)
+                mass = jnp.sum(pd, axis=1, keepdims=True)
+                acc = nn(pd.astype(BF), v_s[rs, cs])
+                if i:
+                    po = jnp.exp(so - top)
+                    mass = mass + jnp.sum(po, axis=1, keepdims=True)
+                    acc = acc + nn(po.astype(BF), v_s[before, cs])
+                parts.append(acc * (1.0 / mass))
+                lse_s[rs, :] = jnp.where(lane == 2 * j + h, top + jnp.log(mass), lse_s[rs, :])
+            o_s[rs, cs] = jnp.where(lane < 64, parts[0], parts[1]).astype(BF)
+        return carry
+
+    lse_s[...] = jnp.zeros_like(lse_s)
+    lax.fori_loop(0, 6, pair, 0)
+    store(o_s, o_out)
+    store(lse_s, lse_out)
+    for copy in kept:
+        copy.wait()
+    h2_s, h2t_s, dxb_s, do_s = q_s, h1t_s, k_s, v_s
+    gain2 = gains[1:2, :]
+
+    def middle(r, carry):
+        rs = pl.ds(pl.multiple_of(r * 256, 256), 256)
+        x2 = x_ref[rs, :].astype(F32) + nn(o_s[rs, :], flat(wo_s[...]))
+        x2_s[rs, :] = x2
+        h2 = (x2 * lax.rsqrt(jnp.mean(x2 * x2, axis=1, keepdims=True) + EPS) * gain2).astype(BF)
+        h2_s[rs, :] = h2
+        h2t_s[:, rs] = h2.T
+        return carry
+
+    lax.fori_loop(0, blocks, middle, 0)
+
+    def swap(buf, width, got, k):
+        far = pl.ds(pl.multiple_of((1 - pc.c) * width, 128), width)
+        return remote(buf.at[..., far], got, rsend.at[k], rrecv.at[k], pc.other)
+
+    def near(buf, width):
+        return buf[..., pl.ds(pl.multiple_of(pc.c * width, 128), width)]
+
+    gu_swap = [swap(gu_st.at[u % 2], 512, gu_r.at[u], u) for u in range(4)]
+    d_swap = [swap(d_st.at[u % 2], 384, d_r.at[u], 4 + u) for u in range(4)]
+
+    def settle(u):
+        gu_swap[u].wait_recv()
+        d_swap[u].wait_recv()
+        for z in range(4):
+            mine = gu_st[u % 2, z, :, :, pl.ds(pl.multiple_of(pc.c * 512, 128), 512)]
+            gu_r[u, z] = (gu_r[u, z].astype(F32) + mine.astype(F32)).astype(BF)
+        mine = d_st[u % 2, :, :, pl.ds(pl.multiple_of(pc.c * 384, 128), 384)]
+        d_r[u] = (d_r[u].astype(F32) + mine.astype(F32)).astype(BF)
+        store(gu_r.at[u], gu_sum.at[u])
+        store(d_r.at[u], d_sum.at[u])
+        gu_swap[u].wait_send()
+        d_swap[u].wait_send()
+
+    for u in range(4):
+        run_all(slots[8 + u])
+        wgu = pl.ds(u * 1024, 1024)
+
+        def mix(r, carry):
+            rs = pl.ds(pl.multiple_of(r * 256, 256), 256)
+            both = nn(h2_s[rs, :], flat(wgu_s[:, :, :, wgu]))
+            dhid = nt(dy_ref[rs, :], flat(wd_s[u]))
+            hids, grads = [], []
+            for n in range(2):
+                gate, up = both[:, n * 512 : n * 512 + 256], both[:, n * 512 + 256 : n * 512 + 512]
+                dh = dhid[:, n * 256 : n * 256 + 256]
+                sig = sigmoid(gate)
+                silu = gate * sig
+                hids.append((silu * up).astype(BF))
+                grads.append((dh * up * sig * (1.0 + gate * (1.0 - sig))).astype(BF))
+                grads.append((dh * silu).astype(BF))
+            hid = jnp.concatenate(hids, axis=1)
+            dgu = jnp.concatenate(grads, axis=1)
+            hidt_s[:, rs] = hid.T
+            dgu_s[rs, :] = dgu
+            yv = nn(hid, flat(wd_s[u]))
+            dv = nt(dgu, flat(wgu_s[:, :, :, wgu]))
+            if u == 0:
+                y_s[rs, :] = x2_s[rs, :] + yv
+                dh2_s[rs, :] = dv
+            else:
+                y_s[rs, :] += yv
+                dh2_s[rs, :] += dv
+            return carry
+
+        lax.fori_loop(0, blocks, mix, 0)
+        if u >= 2:
+            settle(u - 2)
+
+        def weight_gu(z, carry):
+            rows = nn(h2t_s[pl.ds(pl.multiple_of(z * 192, 64), 192), :], dgu_s[...])
+            gu_st[u % 2, z] = rows.astype(BF).reshape(4, 48, 1024)
+            return carry
+
+        lax.fori_loop(0, 4, weight_gu, 0)
+
+        def weight_d(k, carry):
+            rows = nn(hidt_s[pl.ds(pl.multiple_of(k * 256, 256), 256), :], dy_ref[...])
+            d_st[u % 2, pl.ds(k * 2, 2)] = rows.astype(BF).reshape(2, 128, 768)
+            return carry
+
+        lax.fori_loop(0, 2, weight_d, 0)
+        gu_swap[u].start()
+        d_swap[u].start()
+
+    gg_s[...] = jnp.zeros_like(gg_s)
+
+    def back(r, carry):
+        rs = pl.ds(pl.multiple_of(r * 256, 256), 256)
+        yb_s[rs, :] = y_s[rs, :].astype(BF)
+        x2, dh2 = x2_s[rs, :], dh2_s[rs, :]
+        r2 = lax.rsqrt(jnp.mean(x2 * x2, axis=1, keepdims=True) + EPS)
+        n2 = x2 * r2
+        e2 = dh2 * gain2
+        gg_s[0:1, :] += jnp.sum(dh2 * n2, axis=0, keepdims=True)
+        dx2 = dy_ref[rs, :].astype(F32) + r2 * (e2 - n2 * jnp.mean(e2 * n2, axis=1, keepdims=True))
+        x2_s[rs, :] = dx2
+        dxb = dx2.astype(BF)
+        dxb_s[rs, :] = dxb
+        do_s[rs, :] = nt(dxb, flat(wo_s[...])).astype(BF)
+        h2t_s[:, rs] = o_s[rs, :].T
+        return carry
+
+    lax.fori_loop(0, blocks, back, 0)
+    store(yb_s, y_out)
+    store(x2_s, dx2_out)
+    store(do_s, do_out)
+    store(gg_s, gg_out)
+    settle(2)
+
+    def weight_o(z, carry):
+        rows = nn(h2t_s[pl.ds(pl.multiple_of(z * 192, 64), 192), :], dxb_s[...])
+        o_st[z] = rows.astype(BF).reshape(4, 48, 768)
+        return carry
+
+    lax.fori_loop(0, 4, weight_o, 0)
+    o_swap = swap(o_st, 384, o_r, 8)
+    o_swap.start()
+    settle(3)
+    o_swap.wait_recv()
+    mine = o_st[:, :, :, pl.ds(pl.multiple_of(pc.c * 384, 128), 384)]
+    o_r[...] = (o_r[...].astype(F32) + mine.astype(F32)).astype(BF)
+    store(o_r, o_sum)
+    o_swap.wait_send()
+    for copy in gain_copies:
+        copy.wait_send()
+    for copy in outs:
+        if not any(copy is done for done in kept):
+            copy.wait()
+
+
+class Reduce:
+    def __init__(self, place, keep, r1, r2, r3, total, other_total, send, recv, far1, far2, near):
+        pc = place
+        self.pc, self.keep, self.r1, self.r2, self.r3, self.total = pc, keep, r1, r2, r3, total
+        self.to_first = [remote(ref, r1.at[:, i], send.at[i], recv.at[i], pc.first) for i, ref in enumerate((far1, far2))]
+        self.near = near
+        self.to_second = remote(keep.at[:, 1], r2, send.at[2], recv.at[2], pc.second)
+        self.zs = [remote(keep.at[pc.z_at(d), 0], r3.at[d - 1], send.at[2 + d], recv.at[2 + d], pc.z_dev(d)) for d in (1, 2, 3)]
+        self.to_core = remote(total, other_total, send.at[6], recv.at[6], pc.other)
+
+    def steps(self, begin, finish):
+        pc = self.pc
+
+        def r1():
+            begin()
+            for copy in self.to_first:
+                copy.start()
+
+        def r2():
+            for copy in self.near:
+                copy.wait()
+            for copy in self.to_first:
+                copy.wait_recv()
+
+            def add(z, carry):
+                self.keep[z] = (self.keep[z].astype(F32) + self.r1[z].astype(F32)).astype(BF)
+                return carry
+
+            lax.fori_loop(0, 4, add, 0)
+            self.to_second.start()
+
+        def r3():
+            self.to_second.wait_recv()
+
+            def add(z, carry):
+                self.keep[z, 0] = (self.keep[z, 0].astype(F32) + self.r2[z].astype(F32)).astype(BF)
+                return carry
+
+            lax.fori_loop(0, 4, add, 0)
+            for copy in self.zs:
+                copy.start()
+
+        def r4():
+            for copy in self.zs:
+                copy.wait_recv()
+            total = self.keep[pc.z, 0].astype(F32)
+            for d in range(3):
+                total = total + self.r3[d].astype(F32)
+            self.total[...] = total
+            self.to_core.start()
+
+        def r5():
+            self.to_core.wait()
+            finish()
+            for copy in [*self.to_first, self.to_second, *self.zs]:
+                copy.wait_send()
+
+        return [r1, r2, r3, r4, r5]
+
+
+def hind_kernel(
+    q_hbm, k_hbm, v_hbm, o_hbm, do_hbm, lse_hbm, seg_hbm, rope_hbm, h1t_hbm, w_hbm, x_hbm, dx2_hbm, gain_ref, gg_ref, gu_sum, d_sum, o_sum,
+    gx_ref, gwq, gwk, gwv, gwo, gwg, gwu, gwd, gg_out,
+    q_s, k_s, v_s, o_s, do_s, lse_s, seg_s, rope_s, h1t_s, w_s, x_s, dx2_s, dqkv_s, dk_s, dv_s,
+    gq_s, gq_r, gu_k, gu_1, gu_2, gu_3, gu_t, d_k, d_1, d_2, d_3, d_t, o_k, o_1, o_2, o_3, o_t, qk_k, qk_1, qk_2, qk_3, qk_t,
+    gg1_s, gg_st, gg_r, gg_c,
+    lsem, nsem, ssend, srecv, qsend, qrecv, gsend, grecv,
+):
+    pc = Place()
+    tok = x_s.shape[0]
+    blocks = tok // 256
+    loads = []
+
+    def load(src, dst):
+        copy = pltpu.make_async_copy(src, dst, lsem.at[len(loads)])
+        copy.start()
+        loads.append(copy)
+        return copy
+
+    for src, dst in ((q_hbm, q_s), (k_hbm, k_s), (v_hbm, v_s), (o_hbm, o_s), (do_hbm, do_s), (lse_hbm, lse_s), (seg_hbm, seg_s), (rope_hbm, rope_s)):
+        load(src, dst)
+    early = len(loads)
+    for src, dst in ((h1t_hbm, h1t_s), (w_hbm, w_s), (x_hbm, x_s), (dx2_hbm, dx2_s)):
+        load(src, dst)
+    enter(pc)
+
+    nears = []
+
+    def start_near(copies):
+        for copy in copies:
+            copy.start()
+
+    def unit(n, parts, keep, r1, r2, r3, total, finish, source=None):
+        near = []
+        if source is None:
+            near = [pltpu.make_async_copy(parts(q), keep.at[:, i], nsem.at[n, i]) for i, q in enumerate((pc.p, pc.q2))]
+        red = Reduce(pc, keep, r1, r2, r3, total.at[0], total.at[1], ssend.at[n], srecv.at[n], parts(pc.q1), parts(pc.q3), near)
+
+        def begin():
+            if source is not None:
+                source()
+            start_near(near)
+
+        return red.steps(begin, finish)
+
+    def halves(ref):
+        mine, others = ref[0], ref[1]
+        zero = pc.c == 0
+        return jnp.where(zero, mine, others), jnp.where(zero, others, mine)
+
+    units = []
+    for u in range(4):
+
+        def finish_gu(u=u):
+            low, high = halves(gu_t.at[u])
+            for n, part in enumerate((low, high)):
+                gwg[:, pl.ds(u * 512 + n * 256, 256)] = part[:, :256]
+                gwu[:, pl.ds(u * 512 + n * 256, 256)] = part[:, 256:]
+
+        units.append(unit(u, lambda q, u=u: gu_sum.at[u, :, q], gu_k.at[u], gu_1.at[u], gu_2.at[u], gu_3.at[u], gu_t.at[u], finish_gu))
+
+    def finish_o():
+        low, high = halves(o_t)
+        gwo[:, 0:384] = low
+        gwo[:, 384:768] = high
+
+    units.append(unit(4, lambda q: o_sum.at[:, q], o_k, o_1, o_2, o_3, o_t, finish_o))
+
+    def finish_d():
+        low, high = halves(d_t)
+        gwd[:, 0:384] = low
+        gwd[:, 384:768] = high
+
+    units.append(unit(5, lambda q: d_sum.at[:, q], d_k, d_1, d_2, d_3, d_t, finish_d))
+
+    q_swaps = [remote(gq_s.at[2 * m + 1 - pc.c], gq_r.at[m], qsend.at[m], qrecv.at[m], pc.other) for m in range(3)]
+
+    for m in range(3):
+
+        def finish_q(m=m):
+            low, high = halves(qk_t.at[m])
+            for n, part in enumerate((low, high)):
+                cs = pl.ds((2 * m + n) * 128, 128)
+                gwq[:, cs] = part[:, 0:128]
+                gwk[:, cs] = part[:, 128:256]
+                gwv[:, cs] = part[:, 256:384]
+
+        def source(m=m):
+            q_swaps[m].wait_recv()
+            mine = 2 * m + pc.c
+
+            def add(z, carry):
+                got = gq_r[m, z]
+                gq_r[m, z] = (got.astype(F32) + gq_s[mine, z].astype(F32)).astype(BF)
+                return carry
+
+            lax.fori_loop(0, 4, add, 0)
+            for i, q in enumerate((pc.p, pc.q2)):
+                qk_k[m, :, i] = gq_r[m, :, q]
+            q_swaps[m].wait_send()
+
+        units.append(unit(6 + m, lambda q, m=m: gq_r.at[m, :, q], qk_k.at[m], qk_1.at[m], qk_2.at[m], qk_3.at[m], qk_t.at[m], finish_q, source))
+    slots = fold(units)
+    ticks = {0: 0, 1: 1, 3: 2, 4: 3, 6: 4, 7: 5, 9: 6, 11: 7}
+
+    run_all(slots[0])
+    for copy in loads[:early]:
+        copy.wait()
+    ones = (lane_of(tok) < 3).astype(BF)
+
+    def pair(j, carry):
+        cs = pl.ds(pl.multiple_of(j * 128, 128), 128)
+        lane = lane_of(256)
+        above = lax.broadcasted_iota(jnp.int32, (256, 256), 0) <= lax.broadcasted_iota(jnp.int32, (256, 256), 1)
+        at = pair_at(j)
+        dk_s[...] = jnp.zeros_like(dk_s)
+        dv_s[...] = jnp.zeros_like(dv_s)
+        vaug = jnp.concatenate([v_s[:, cs], ones], axis=1)
+        kaug = jnp.concatenate([k_s[:, cs], seg_s[1]], axis=1)
+        kt = k_s[:, cs].T
+        for i in range(blocks):
+            if i in (1, 3):
+                for tick, slot in ticks.items():
+                    if slot and tick % 2 == i // 2:
+                        pl.when(j == tick // 2)(functools.partial(run_all, slots[slot]))
+            rs, first, last = pl.ds(i * 256, 256), i * 256, (i + 1) * 256
+            qt, dt = q_s[rs, cs], do_s[rs, cs]
+            prod = dt.astype(F32) * o_s[rs, cs].astype(F32)
+            parts = []
+            for h in range(2):
+                mask = (lane < 64) == (h == 0)
+                qm, dm = jnp.where(mask, qt, BF(0)), jnp.where(mask, dt, BF(0))
+                delta = jnp.sum(jnp.where(mask, prod, 0.0), axis=1, keepdims=True)
+                lse = jnp.sum(jnp.where(lane == 2 * j + h, lse_s[rs, :], 0.0), axis=1, keepdims=True)
+                a0, a1, a2 = three_way(-lse)
+                qa = jnp.where(lane == 4, a0, jnp.where(lane == 5, a1, jnp.where(lane == 6, a2, seg_s[0, rs, :])))
+                b0, b1, b2 = three_way(-delta)
+                da = jnp.where(lane == 0, b0, jnp.where(lane == 1, b1, jnp.where(lane == 2, b2, BF(0))))
+                qaug, daug = jnp.concatenate([qm, qa], axis=1), jnp.concatenate([dm, da], axis=1)
+                pd = jnp.exp(jnp.where(above, nt(kaug[first:last], qaug), NEG))
+                dsd = (pd * nt(vaug[first:last], daug)).astype(BF)
+                dv_s[rs, :] += nn(pd.astype(BF), dm)
+                dk_s[rs, :] += nn(dsd, qm)
+                dq = nn(kt[h * 64 : h * 64 + 64, first:last], dsd)
+                if i:
+                    before = pl.ds(0, first)
+                    po = jnp.exp(nt(kaug[:first], qaug))
+                    dso = (po * nt(vaug[:first], daug)).astype(BF)
+                    dv_s[before, :] += nn(po.astype(BF), dm)
+                    dk_s[before, :] += nn(dso, qm)
+                    dq = dq + nn(kt[h * 64 : h * 64 + 64, :first], dso)
+                parts.append(dq)
+            dq = jnp.concatenate(parts, axis=0).T * 0.125
+            dq = dq * rope_s[0, rs, :] + turned(dq * rope_s[1, rs, :], lane, True)
+            dqkv_s[rs, pl.ds(pl.multiple_of(at, 128), 128)] = dq.astype(BF)
+
+        def finish(r, carry):
+            rs = pl.ds(pl.multiple_of(r * 256, 256), 256)
+            dk = dk_s[rs, :]
+            dk = dk * rope_s[0, rs, :] + turned(dk * rope_s[1, rs, :], lane, True)
+            dqkv_s[rs, pl.ds(pl.multiple_of(at + 128, 128), 128)] = dk.astype(BF)
+            dqkv_s[rs, pl.ds(pl.multiple_of(at + 256, 128), 128)] = dv_s[rs, :].astype(BF)
+            return carry
+
+        lax.fori_loop(0, blocks, finish, 0)
+        pl.when(j == 0)(loads[early].wait)
+
+        def weight(z, carry):
+            rows = nn(h1t_s[pl.ds(pl.multiple_of(z * 192, 64), 192), :], dqkv_s[:, pl.ds(pl.multiple_of(at, 128), 384)])
+            gq_s[j, z] = rows.astype(BF).reshape(4, 48, 384)
+            return carry
+
+        lax.fori_loop(0, 4, weight, 0)
+        for m in range(3):
+            pl.when((j // 2 == m) & (lax.rem(j, 2) != pc.c))(q_swaps[m].start)
+        return carry
+
+    lax.fori_loop(0, 6, pair, 0)
+    run_all(slots[8])
+    for copy in loads[early + 1 :]:
+        copy.wait()
+    gg1_s[...] = jnp.zeros_like(gg1_s)
+    gain1 = gain_ref[0:1, :]
+
+    def last(r, carry):
+        rs = pl.ds(pl.multiple_of(r * 256, 256), 256)
+        dh1 = nt(dqkv_s[rs, :], flat(w_s[...]))
+        x = x_s[rs, :].astype(F32)
+        r1 = lax.rsqrt(jnp.mean(x * x, axis=1, keepdims=True) + EPS)
+        n1 = x * r1
+        e1 = dh1 * gain1
+        gg1_s[0:1, :] += jnp.sum(dh1 * n1, axis=0, keepdims=True)
+        gx_ref[rs, :] = (dx2_s[rs, :] + r1 * (e1 - n1 * jnp.mean(e1 * n1, axis=1, keepdims=True))).astype(BF)
+        for t in range(4):
+            pl.when(r == t)(functools.partial(run_all, slots[9 + t]))
+        return carry
+
+    lax.fori_loop(0, blocks, last, 0)
+    row = lax.broadcasted_iota(jnp.int32, (16, 768), 0)
+    terms = jnp.zeros((16, 768), BF)
+    for n, sums in enumerate((gg1_s, gg_ref)):
+        for k, term in enumerate(three_way(sums[0:1, :])):
+            terms = jnp.where(row == 8 * n + k, term, terms)
+
+    def cut(w, carry):
+        gg_st[w] = nt(terms, spread(w))
+        return carry
+
+    lax.fori_loop(0, 16, cut, 0)
+    copies = []
+    for d in range(1, 16):
+        to = lax.rem(pc.w + d, 16)
+        copy = remote(gg_st.at[to], gg_r.at[d - 1], gsend.at[d - 1], grecv.at[d - 1], {"wide": to})
+        copy.start()
+        copies.append(copy)
+    total = gg_st[pc.w]
+    for d in range(1, 16):
+        copies[d - 1].wait_recv()
+        total = total + gg_r[d - 1]
+    gg_c[0] = total
+    to_core = remote(gg_c.at[0], gg_c.at[1], gsend.at[15], grecv.at[15], pc.other)
+    to_core.start()
+    to_core.wait()
+    gg_out[...] = gg_c[0] + gg_c[1]
+    for copy in copies:
+        copy.wait_send()
+
+
+def shape(dims, dtype=BF):
+    return jax.ShapeDtypeStruct(dims, dtype)
+
+
+def fast_body(tokens, seq_lengths, w_query, w_key, w_value, w_out, w_gate, w_up, w_down, attn_gain, ffn_gain, cotangent):
+    tok, width = tokens.shape
+    any_spec, vmem_spec = pl.BlockSpec(memory_space=pl.ANY), pl.BlockSpec(memory_space=pltpu.VMEM)
+    dma = pltpu.SemaphoreType.DMA
+    vm = pltpu.VMEM
+    tile = jnp.pad(jnp.stack([attn_gain, ffn_gain]), ((0, 14), (0, 128 - attn_gain.shape[0])))
+    fore = pl.pallas_call(
+        fore_kernel,
+        out_shape=[
+            shape((tok, width)), shape((tok, width)), shape((tok, width)), shape((tok, width)), shape((tok, width)),
+            shape((width, tok)), shape((tok, 128), F32), shape((2, tok, 128)), shape((2, tok, 128), F32),
+            shape((4, 4, 48, 2304)), shape((tok, width), F32), shape((16, width), F32), shape((8, width), F32), shape((tok, width)),
+            shape((4, 4, 4, 48, 512)), shape((4, 4, 128, 384)), shape((4, 4, 48, 384)),
+        ],
+        in_specs=[pl.BlockSpec(memory_space=pltpu.SMEM), vmem_spec, vmem_spec] + [any_spec] * 8,
+        out_specs=[any_spec] * 17,
+        scratch_shapes=[
+            vm((4, 4, 48, 2304), BF), vm((4, 4, 48, 768), BF), vm((4, 4, 48, 4096), BF), vm((4, 4, 128, 768), BF), vm((16, 16, 128), BF), vm((16, width), F32),
+            vm((tok, width), F32), vm((tok, width), F32), vm((tok, width), F32), vm((width, tok), BF),
+            vm((tok, width), BF), vm((tok, width), BF), vm((tok, width), BF), vm((tok, width), BF),
+            vm((tok, 128), F32), vm((2, tok, 128), BF), vm((2, tok, 128), F32),
+            vm((512, tok), BF), vm((tok, 1024), BF), vm((8, width), F32), vm((tok, width), BF),
+            vm((2, 4, 4, 48, 1024), BF), vm((2, 4, 128, 768), BF), vm((4, 4, 48, 768), BF),
+            vm((4, 4, 4, 48, 512), BF), vm((4, 4, 128, 384), BF), vm((4, 4, 48, 384), BF),
+            dma((31,)), dma((31,)), dma((7, 10)), dma((7, 10)), dma((15,)), dma((15,)), dma((9,)), dma((9,)), dma((20,)), dma((24,)),
+        ],
+        compiler_params=pltpu.CompilerParams(collective_id=0, has_side_effects=True, vmem_limit_bytes=VMEM_BYTES),
+        name="fore",
+    )
+    (q, k, v, o, do, h1t, lse, seg, rope, wqkv, dx2, gains, gg2, output, gu_sum, d_sum, o_sum) = fore(
+        seq_lengths, tokens, cotangent, tile, w_query, w_key, w_value, w_out, w_gate, w_up, w_down
+    )
+    hind = pl.pallas_call(
+        hind_kernel,
+        out_shape=[shape((tok, width))] + [shape((48, width), F32)] * 4 + [shape((48, 2048), F32)] * 2 + [shape((128, width), F32), shape((16, 128), F32)],
+        in_specs=[any_spec] * 12 + [vmem_spec] * 2 + [any_spec] * 3,
+        out_specs=[vmem_spec] * 9,
+        scratch_shapes=[
+            vm((tok, width), BF), vm((tok, width), BF), vm((tok, width), BF), vm((tok, width), BF), vm((tok, width), BF),
+            vm((tok, 128), F32), vm((2, tok, 128), BF), vm((2, tok, 128), F32), vm((width, tok), BF), vm((4, 4, 48, 2304), BF),
+            vm((tok, width), BF), vm((tok, width), F32), vm((tok, 2304), BF), vm((tok, 128), F32), vm((tok, 128), F32),
+            vm((6, 4, 4, 48, 384), BF), vm((3, 4, 4, 48, 384), BF),
+            vm((4, 4, 2, 48, 512), BF), vm((4, 4, 2, 48, 512), BF), vm((4, 4, 48, 512), BF), vm((4, 3, 48, 512), BF), vm((4, 2, 48, 512), F32),
+            vm((4, 2, 128, 384), BF), vm((4, 2, 128, 384), BF), vm((4, 128, 384), BF), vm((3, 128, 384), BF), vm((2, 128, 384), F32),
+            vm((4, 2, 48, 384), BF), vm((4, 2, 48, 384), BF), vm((4, 48, 384), BF), vm((3, 48, 384), BF), vm((2, 48, 384), F32),
+            vm((3, 4, 2, 48, 384), BF), vm((3, 4, 2, 48, 384), BF), vm((3, 4, 48, 384), BF), vm((3, 3, 48, 384), BF), vm((3, 2, 48, 384), F32),
+            vm((8, width), F32), vm((16, 16, 128), F32), vm((15, 16, 128), F32), vm((2, 16, 128), F32),
+            dma((12,)), dma((6, 2)), dma((9, 7)), dma((9, 7)), dma((3,)), dma((3,)), dma((16,)), dma((16,)),
+        ],
+        compiler_params=pltpu.CompilerParams(collective_id=1, has_side_effects=True, vmem_limit_bytes=VMEM_BYTES),
+        name="hind",
+    )
+    gx, gwq, gwk, gwv, gwo, gwg, gwu, gwd, gg = hind(q, k, v, o, do, lse, seg, rope, h1t, wqkv, tokens, dx2, gains, gg2, gu_sum, d_sum, o_sum)
+    count = attn_gain.shape[0]
+    return (output, gx, gwq, gwk, gwv, gwo, gwg, gwu, gwd, gg[0:3, :count].sum(axis=0), gg[8:11, :count].sum(axis=0))
 
 
 def layout(lengths, tok_count):
-    seq_ends = jnp.cumsum(lengths)
+    slots = jnp.arange(lengths.shape[0])
+    seq_ends = jnp.sum(jnp.where(slots[:, None] <= slots[None, :], lengths[:, None], 0), axis=0)
     starts = seq_ends - lengths
     places = jnp.arange(tok_count, dtype=jnp.int32)
     segment = jnp.sum((places[:, None] >= seq_ends[None, :]).astype(jnp.int32), axis=1)
@@ -123,7 +969,7 @@
     return (jnp.concatenate(grad_queries, axis=0), grad_keys, grad_values)
 
 
-def body(
+def plain_body(
     tokens,
     seq_lengths,
     w_query,
@@ -190,30 +1036,6 @@
     hidden = swiglu(gate, upward).astype(jnp.bfloat16)
     result = middle + jnp.dot(hidden, full_down, preferred_element_type=jnp.float32)
     output = result.astype(jnp.bfloat16)
-    again = (
-        lax.all_gather(w_query, "wide", axis=0, tiled=True),
-        lax.all_gather(w_key, "wide", axis=0, tiled=True),
-        lax.all_gather(w_value, "wide", axis=0, tiled=True),
-        lax.all_gather(w_out, "wide", axis=0, tiled=True),
-        lax.all_gather(w_gate, "wide", axis=0, tiled=True),
-        lax.all_gather(w_up, "wide", axis=0, tiled=True),
-        lax.all_gather(w_down, "wide", axis=0, tiled=True),
-        lax.all_gather(attn_gain, "wide", axis=0, tiled=True),
-        lax.all_gather(ffn_gain, "wide", axis=0, tiled=True),
-    )
-    (
-        full_query,
-        full_key,
-        full_value,
-        full_out,
-        full_gate,
-        full_up,
-        full_down,
-        gain_one,
-        gain_two,
-    ) = again
-    gain_one = gain_one.astype(jnp.float32)
-    gain_two = gain_two.astype(jnp.float32)
     grad_out_rows = cotangent.astype(jnp.float32)
     grad_down = outer_sum(hidden, cotangent)
     grad_hidden = back_dot(cotangent, full_down)
@@ -317,4 +1139,6 @@
         P("wide"),
         P("wide"),
     )
+    blocks = (mesh.shape["wide"], mesh.shape["narrow"]) == (16, 2)
+    body = fast_body if blocks else plain_body
     return jax.shard_map(body, mesh=mesh, in_specs=in_specs, out_specs=out_specs, check_vma=False)

time: 1550 us -> 246 us (0.16)
  waiting for transfers between devices: 1060 us -> 0 us
  matrix products: 245 us -> 0 us
  Pallas kernels: 0 us -> 234 us
  other arithmetic: 107 us -> 2.48 us
  blocking collectives: 86.7 us -> 0 us
  local copies, waits for them, and re-layouts: 31.6 us -> 8.03 us
  between operations: 16.4 us -> 0.69 us
    reduce_scatter x7 -> x0, waiting for transfers between devices: 780 us -> none  [the longest x1 149 us: body(): lax.psum_scatter(grad_gate, 'wide', scatter_dimension=0, tiled=True)]
    all_gather x7 -> x0, waiting for transfers between devices: 271 us -> none  [the longest x1 63.1 us: body(): lax.all_gather(w_up, 'wide', axis=0, tiled=True)]
    dot_general x33 -> x0, matrix products: 245 us -> none  [the longest x7 44.2 us: back_dot(): lax.dot_general(rows_in, weight, (((1,), (1,)), ((), ())), preferred_elem...]
    pallas_call x0 -> x2, Pallas kernels: none -> 234 us  [the longest x1 136 us: fast_body(): fore(seq_lengths, tokens, cotangent, tile, w_query, w_key, w_value, w_out...]
    unnamed x2 -> x0, blocking collectives: 84.2 us -> none
    convert_element_type x25 -> x0, other arithmetic: 75.1 us -> none  [the longest x1 42.2 us: attend_backward(): grad_scores = (probs * (grad_probs - inner)).astype(jnp.bfloat16)]
    unnamed x111 -> x27, local copies, waits for them, and re-layouts: 30.3 us -> 8.03 us
    reduce_sum x5 -> x1, other arithmetic: 19.8 us -> 1.21 us  [fast_body(): gg[8:11, :count].sum(axis=0)]
  transfers between devices with their start and end apart: 15 -> 0, of which waited for: 12 -> 0; matrix products, arithmetic and copies ran while one was open for 20% -> 0% of each run, Pallas kernels for 0% -> 0%
where the time goes in v1:
time: 246 us
  Pallas kernels  234 us (95%)
  local copies, waits for them, and re-layouts  8.03 us (3%)
  other arithmetic  2.48 us (1%)
    pallas_call x1, Pallas kernels, fast_body(): fore(seq_lengths, tokens, cotangent, tile, w_query, w_key, w_value, w_out...  136 us
    pallas_call x1, Pallas kernels, fast_body(): hind(q, k, v, o, do, lse, seg, rope, h1t, wqkv, tokens, dx2, gains, gg2,...  98.7 us
    unnamed x27, local copies, waits for them, and re-layouts  8.03 us

profile of v1, /device:TPU:0, one launch (start us, length us, event | category | flops | bytes accessed | tf_op | source)
XLA Modules:
  0.0 245.6 jit_solution(11957113835478267570)
XLA Ops:
  0.6 1.3 fusion.5.gt_hbm
  1.9 135.6 %fore.1 = (bf16[1024,768]{1,0:T(8,128)(2,1)}, bf16[1024,768]{1,0:T(8,128)(2,1)}, bf16[1024,768]{1,0:T(8,128)(2,1)}, bf16[1024,768]{1,0:T(8,128)(2,1)}, bf16[1024...) custom-call(s32[1,4]{1,0:T(1,128)} %lens.1, ...), custom_call_target="tpu_custom_call" | custom-call | tf_op jit(solution)/shard_map/fore/pallas_call | solution.py:831
  137.6 0.0 copy-start
  137.6 98.7 %hind.1 = (bf16[1024,768]{1,0:T(8,128)(2,1)}, f32[48,768]{1,0:T(8,128)}, f32[48,768]{1,0:T(8,128)}, f32[48,768]{1,0:T(8,128)}, f32[48,768]{1,0:T(8,128)}, /*inde...) custom-call(bf16[1024,768]{1,0:T(8,128)(2,1)} %get-tuple-element.38.q_hbm, ...), custom_call_target="tpu_custom_call" | custom-call | tf_op jit(solution)/shard_map/hind/pallas_call | solution.py:854
  236.3 1.2 slice_reduce_fusion
  237.5 0.0 copy-done
  237.5 0.0 copy-start.1
  237.5 1.1 copy.32
  238.7 0.8 copy-done.1
  239.5 0.0 copy-start.8
  239.5 0.0 copy-start.7
  239.5 0.0 copy-start.6
  239.5 0.0 copy-start.5
  239.5 0.0 copy-start.4
  239.5 1.1 copy.33
  240.7 0.0 copy-done.8
  240.7 0.0 copy-start.3
  240.7 0.0 copy-start.2
  240.7 0.7 copy.34
  241.3 0.0 copy-done.7
  241.3 0.7 copy.35
  242.0 0.0 copy-done.6
  242.0 0.7 copy.36
  242.7 0.0 copy-done.5
  242.7 0.7 copy.37
  243.3 0.0 copy-done.4
  243.3 0.7 copy.38
  244.1 0.0 copy-done.3
  244.1 0.7 copy.39
  244.8 0.0 copy-done.2
  244.8 0.7 copy.40
Async XLA Ops:
  137.6 99.9 %copy-start = (bf16[1024,768]{1,0:T(8,128)(2,1)S(1)}, bf16[1024,768]{1,0:T(8,128)(2,1)}, u32[]{:S(2)}) copy-start(bf16[1024,768]{1,0:T(8,128)(2,1)} %get-tuple-element.76) | copy-start | bytes 4718596
  237.5 2.0 copy-start.1
  239.5 1.2 copy-start.8
  239.5 1.8 copy-start.7
  239.5 2.5 %copy-start.6 = (f32[48,768]{1,0:T(8,128)S(1)}, f32[48,768]{1,0:T(8,128)}, u32[]{:S(2)}) copy-start(f32[48,768]{1,0:T(8,128)} %get-tuple-element.80) | copy-start | bytes 442372
  239.5 3.2 %copy-start.5 = (f32[48,768]{1,0:T(8,128)S(1)}, f32[48,768]{1,0:T(8,128)}, u32[]{:S(2)}) copy-start(f32[48,768]{1,0:T(8,128)} %get-tuple-element.81) | copy-start | bytes 442372
  239.5 3.8 %copy-start.4 = (f32[48,2048]{1,0:T(8,128)S(1)}, f32[48,2048]{1,0:T(8,128)}, u32[]{:S(2)}) copy-start(f32[48,2048]{1,0:T(8,128)} %get-tuple-element.82) | copy-start | bytes 1179652
  240.7 3.4 %copy-start.3 = (f32[48,2048]{1,0:T(8,128)S(1)}, f32[48,2048]{1,0:T(8,128)}, u32[]{:S(2)}) copy-start(f32[48,2048]{1,0:T(8,128)} %get-tuple-element.83) | copy-start | bytes 1179652
  240.7 4.2 %copy-start.2 = (f32[128,768]{1,0:T(8,128)S(1)}, f32[128,768]{1,0:T(8,128)}, u32[]{:S(2)}) copy-start(f32[128,768]{1,0:T(8,128)} %get-tuple-element.84) | copy-start | bytes 1179652

commit v2 on v1

--- a/solution.py
+++ b/solution.py
@@ -38,6 +38,24 @@
     rest = v - high.astype(F32)
     mid = rest.astype(BF)
     return high, mid, (rest - mid.astype(F32)).astype(BF)
+
+
+FORE = [
+    ("enter", "Q.s0"), ("Q1", "Q.a0 Q.b0"), ("Q2", "Q.p3 Q.b3 Q.a3 Q.p2"),
+    ("Q3", "Q.a2 D0.s0 Q.d3"), ("Q3", "Q.p1 Q.d0 Q.d2 O.s0"), ("Q3", "Q.b2 Q.a1 Q.b1 Q.d1"), ("Q3", "D0.s1 Q.s5"),
+    ("P.2", "O.s1"), ("P.3", "D1.s0"), ("A0.2", "O.s2"), ("A1.0", "G0.s0"), ("A1.3", "D1.s1"), ("A2.2", "G1.s0"), ("A2.3", "G0.s1"),
+    ("A3.1", "O.s3"), ("A3.2", "O.s4 D0.s2"), ("A4.0", "D1.s2 D0.s3"), ("A4.2", "G2.s0 G0.s2"), ("A5.1", "D0.s4"), ("A5.2", "G1.s1"),
+    ("A5.3", "D1.s3 O.s5"), ("M.0", "D0.s5 D1.s4"), ("M.0", "G0.s4 G0.s3"), ("M.2", "G2.s1 G3.s0"), ("F0.m0", "G0.s5 D1.s5 G1.s3"), ("F0.m2", "G1.s2"),
+    ("F0.g0", "G3.s1"), ("F0.g2", "G1.s4"), ("F0.g3", "G2.s2"), ("F1.m0", "G1.s5"), ("F1.g0", "G2.s4 G2.s3"), ("F1.g3", "G3.s2"), ("F1.d0", "G3.s3"),
+    ("F2.m0", "G2.s5"), ("F2.m3", "G3.s4"), ("F2.g3", "G3.s5"),
+]
+HIND = [
+    ("enter", "G0.r1 G1.r1"), ("A0.3", "G0.r2 O.r1"), ("W0.0", "G1.r2"), ("A1.0", "D.r1"), ("A1.1", "G0.r3"), ("A1.3", "O.r2"), ("A2.0", "G1.r3 G2.r1"),
+    ("A3.1", "D.r2"), ("A3.2", "O.r3"), ("W3.0", "G2.r2 G3.r1"), ("A4.0", "Q0.r1 D.r3"), ("W4.0", "G2.r3"),
+    ("A5.1", "G3.r2 Q1.r1"), ("A5.2", "Q0.r2"), ("W5.0", "G3.r3"), ("L.0", "Q1.r2"), ("L.1", "Q0.r3"), ("L.2", "Q2.r1 Q1.r3"), ("L.3", "G1.r4"),
+    ("end", "G0.r4 D.r4 Q2.r2"), ("end", "O.r4 Q0.r4 O.r5 G2.r4"), ("end", "Q2.r3 D.r5 Q1.r4 G3.r4"), ("end", "G0.r5 G2.r5 G1.r5 Q0.r5"),
+    ("gains", "G3.r5 Q1.r5 Q2.r4 Q2.r5"),
+]
 
 
 class Place:
@@ -149,7 +167,7 @@
     return [s0, s1, s2, s3, s4, s5]
 
 
-def piece_gather(unit):
+def piece_steps(unit):
     pc = unit.place
     me = pc.c
     planes = (pc.p, pc.q1, pc.q2, pc.q3)
@@ -158,62 +176,69 @@
     second = [unit.copy(7 + d, unit.part(pc.z_at(-d), pc.p, me), pc.second) for d in range(4)]
     onward = [unit.copy(11 + d, unit.part(pc.z_at(-d), pc.q1, me), pc.second) for d in range(4)]
     cores = [[unit.copy(15 + 4 * i + d, unit.part(pc.z_at(-d), q, me), pc.other) for d in range(4)] for i, q in enumerate(planes)]
-    for copy in zs:
-        copy.start()
-    first[0].start()
-    second[0].start()
-    cores[0][0].start()
-    order = (0, 1, 3, 2)
-    for n, d in enumerate(order):
-        if n:
-            zs[d - 1].wait_recv()
-            first[d].start()
-            second[d].start()
-            cores[0][d].start()
-        if n:
-            before = order[n - 1]
-            first[before].wait_recv()
-            onward[before].start()
-            cores[1][before].start()
-            second[before].wait_recv()
-            cores[2][before].start()
-    last = order[-1]
-    first[last].wait_recv()
-    onward[last].start()
-    cores[1][last].start()
-    second[last].wait_recv()
-    cores[2][last].start()
-    for d in order:
+
+    def spread_out(d):
+        first[d].start()
+        second[d].start()
+        cores[0][d].start()
+
+    def s0():
+        for copy in zs:
+            copy.start()
+        spread_out(0)
+
+    def p(d):
+        zs[d - 1].wait_recv()
+        spread_out(d)
+
+    def a(d):
+        first[d].wait_recv()
+        onward[d].start()
+        cores[1][d].start()
+
+    def b(d):
+        second[d].wait_recv()
+        cores[2][d].start()
+
+    def c(d):
         onward[d].wait_recv()
         cores[3][d].start()
-    for line in cores:
-        for copy in line:
-            copy.wait_recv()
-    for copy in [*zs, *first, *second, *onward, *sum(cores, [])]:
-        copy.wait_send()
+
+    def s5():
+        for line in cores:
+            for copy in line:
+                copy.wait_recv()
+        for copy in [*zs, *first, *second, *onward, *sum(cores, [])]:
+            copy.wait_send()
+
+    steps = {"s0": s0, "s5": s5}
+    for letter, step in (("p", p), ("a", a), ("b", b), ("d", c)):
+        for d in range(4):
+            steps[f"{letter}{d}"] = functools.partial(step, d)
+    return steps
 
 
 def pair_at(j):
     return lax.rem(j, 2) * 1152 + (j // 2) * 384
 
 
-def fold(units):
-    depth = len(units[0])
-    slots = []
-    for n in range(len(units) + depth - 1):
-        steps = []
-        if n < len(units):
-            steps.append(units[n][0])
-        for s in range(depth - 1, 0, -1):
-            if 0 <= n - s < len(units):
-                steps.append(units[n - s][s])
-        slots.append(steps)
-    return slots
-
-
-def run_all(steps):
-    for step in steps:
-        step()
+class Ticks:
+    def __init__(self, table, steps):
+        self.steps = steps
+        self.table = {}
+        for name, listed in table:
+            self.table[name] = self.table.get(name, []) + listed.split()
+        asked = sum(self.table.values(), [])
+        assert sorted(asked) == sorted(steps), (set(asked) ^ set(steps))
+
+    def at(self, name):
+        for step in self.table.get(name, []):
+            self.steps[step]()
+
+    def when(self, index, names):
+        for k, name in enumerate(names):
+            if name in self.table:
+                pl.when(index == k)(functools.partial(self.at, name))
 
 
 def turned(values, lane, back):
@@ -224,7 +249,7 @@
 
 
 def fore_kernel(
-    lens, x_ref, dy_ref, gt_hbm, wq, wk, wv, wo, wg, wu, wd,
+    lens, x_ref, dy_ref, g1_ref, g2_ref, wq, wk, wv, wo, wg, wu, wd,
     q_out, k_out, v_out, o_out, do_out, h1t_out, lse_out, seg_out, rope_out, w_out, dx2_out, gain_out, gg_out, y_out, gu_sum, d_sum, o_sum,
     w_s, wo_s, wgu_s, wd_s, gain_s, gains, x2_s, y_s, dh2_s, h1t_s, q_s, k_s, v_s, o_s, lse_s, seg_s, rope_s,
     hidt_s, dgu_s, gg_s, yb_s, gu_st, d_st, o_st, gu_r, d_r, o_r,
@@ -243,7 +268,6 @@
     def half(start, width):
         return pl.ds(pl.multiple_of(start + pc.c * width, 128), width)
 
-    load(gt_hbm, gain_s.at[pc.w])
     for m in range(3):
         for n, w in enumerate((wq, wk, wv)):
             load(w.at[:, half(m * 256, 128)], w_s.at[pc.z, pc.p, :, pl.ds(pl.multiple_of(pc.c * 1152 + m * 384 + n * 128, 128), 128)])
@@ -256,13 +280,14 @@
     enter(pc)
     for copy in loads[:early]:
         copy.wait()
+    gain_s[pc.w] = jnp.zeros((8, 128), F32)
+    for n, ref in enumerate((g1_ref, g2_ref)):
+        gain_s[pc.w, n : n + 1, 0 : ref.shape[1]] = ref[...].astype(F32)
     gain_copies = [
         remote(gain_s.at[pc.w], gain_s.at[pc.w], gsend.at[d - 1], grecv.at[d - 1], {"wide": lax.rem(pc.w + d, 16)}) for d in range(1, 16)
     ]
     for copy in gain_copies:
         copy.start()
-    for copy in loads[early:]:
-        copy.wait()
     ends, total = [], jnp.int32(0)
     for s in range(4):
         total = total + lens[0, s]
@@ -286,22 +311,33 @@
         seg_s[1, rs, :] = jnp.where((lane == seg) | ((lane >= 4) & (lane < 7)), 1.0, 0.0).astype(BF)
         return carry
 
-    unit_qkv = Gather(pc, w_s, 0, 1152, (0, 48), wsend, wrecv)
-    lax.fori_loop(0, blocks, tables, 0)
-    piece_gather(unit_qkv)
+    units = {
+        "O": Gather(pc, wo_s, 0, 384, (0, 48), usend.at[0], urecv.at[0]),
+        "D0": Gather(pc, wd_s, 0, 384, (0, 64), usend.at[1], urecv.at[1]),
+        "D1": Gather(pc, wd_s, 0, 384, (64, 64), usend.at[2], urecv.at[2]),
+    }
+    for u in range(4):
+        units[f"G{u}"] = Gather(pc, wgu_s, 1024 * u, 512, (0, 48), usend.at[3 + u], urecv.at[3 + u])
+    steps = {f"Q.{name}": step for name, step in piece_steps(Gather(pc, w_s, 0, 1152, (0, 48), wsend, wrecv)).items() if name != "p0"}
+    for u, unit in units.items():
+        for k, step in enumerate(block_steps(unit)):
+            steps[f"{u}.s{k}"] = step
+    ticks = Ticks(FORE, steps)
+    ticks.at("enter")
+    for copy in loads[early:]:
+        copy.wait()
+    lax.fori_loop(0, blocks // 2, tables, 0)
+    ticks.at("Q1")
+    lax.fori_loop(blocks // 2, blocks, tables, 0)
+    ticks.at("Q2")
     for copy in gain_copies:
         copy.wait_recv()
 
     def gain_rows(w, rows):
-        return rows + nn(gain_s[w], spread(w))
-
-    gains[...] = lax.fori_loop(0, 16, gain_rows, jnp.zeros((16, 768), F32))
-    units = [
-        Gather(pc, wo_s, 0, 384, (0, 48), usend.at[0], urecv.at[0]),
-        Gather(pc, wd_s, 0, 384, (0, 64), usend.at[1], urecv.at[1]),
-        Gather(pc, wd_s, 0, 384, (64, 64), usend.at[2], urecv.at[2]),
-    ] + [Gather(pc, wgu_s, 1024 * u, 512, (0, 48), usend.at[3 + u], urecv.at[3 + u]) for u in range(4)]
-    slots = fold([block_steps(u) for u in units])
+        return rows + nn(gain_s[w].astype(BF), spread(w))
+
+    gains[...] = lax.fori_loop(0, 16, gain_rows, jnp.zeros((8, 768), F32))
+    ticks.at("Q3")
     outs = []
 
     def store(src, dst):
@@ -310,13 +346,13 @@
         outs.append(copy)
         return copy
 
-    run_all(slots[0])
     store(gains, gain_out)
-    w_copy = store(w_s, w_out)
+    store(w_s, w_out)
     store(seg_s, seg_out)
     store(rope_s, rope_out)
 
     def project(r, carry):
+        ticks.when(r, [f"P.{i}" for i in range(4)])
         rs = pl.ds(pl.multiple_of(r * 256, 256), 256)
         lane = lane_of(256)
         x = x_ref[rs, :].astype(F32)
@@ -335,15 +371,13 @@
 
     lax.fori_loop(0, blocks, project, 0)
     kept = [store(q_s, q_out), store(k_s, k_out), store(v_s, v_out), store(h1t_s, h1t_out)]
-    run_all(slots[1])
 
     def pair(j, carry):
-        for t in range(6):
-            pl.when(j == t)(functools.partial(run_all, slots[2 + t]))
         cs = pl.ds(pl.multiple_of(j * 128, 128), 128)
         lane = lane_of(256)
         below = lax.broadcasted_iota(jnp.int32, (256, 256), 0) >= lax.broadcasted_iota(jnp.int32, (256, 256), 1)
         for i in range(blocks):
+            ticks.when(j, [f"A{t}.{i}" for t in range(6)])
             rs, before = pl.ds(i * 256, 256), pl.ds(0, i * 256)
             qt = q_s[rs, cs]
             parts = []
@@ -377,6 +411,7 @@
     gain2 = gains[1:2, :]
 
     def middle(r, carry):
+        ticks.when(r, [f"M.{i}" for i in range(4)])
         rs = pl.ds(pl.multiple_of(r * 256, 256), 256)
         x2 = x_ref[rs, :].astype(F32) + nn(o_s[rs, :], flat(wo_s[...]))
         x2_s[rs, :] = x2
@@ -411,10 +446,10 @@
         d_swap[u].wait_send()
 
     for u in range(4):
-        run_all(slots[8 + u])
         wgu = pl.ds(u * 1024, 1024)
 
         def mix(r, carry):
+            ticks.when(r, [f"F{u}.m{i}" for i in range(4)])
             rs = pl.ds(pl.multiple_of(r * 256, 256), 256)
             both = nn(h2_s[rs, :], flat(wgu_s[:, :, :, wgu]))
             dhid = nt(dy_ref[rs, :], flat(wd_s[u]))
@@ -446,6 +481,7 @@
             settle(u - 2)
 
         def weight_gu(z, carry):
+            ticks.when(z, [f"F{u}.g{i}" for i in range(4)])
             rows = nn(h2t_s[pl.ds(pl.multiple_of(z * 192, 64), 192), :], dgu_s[...])
             gu_st[u % 2, z] = rows.astype(BF).reshape(4, 48, 1024)
             return carry
@@ -453,6 +489,7 @@
         lax.fori_loop(0, 4, weight_gu, 0)
 
         def weight_d(k, carry):
+            ticks.when(k, [f"F{u}.d{i}" for i in range(2)])
             rows = nn(hidt_s[pl.ds(pl.multiple_of(k * 256, 256), 256), :], dy_ref[...])
             d_st[u % 2, pl.ds(k * 2, 2)] = rows.astype(BF).reshape(2, 128, 768)
             return carry
@@ -617,7 +654,7 @@
         zero = pc.c == 0
         return jnp.where(zero, mine, others), jnp.where(zero, others, mine)
 
-    units = []
+    units = {}
     for u in range(4):
 
         def finish_gu(u=u):
@@ -626,21 +663,21 @@
                 gwg[:, pl.ds(u * 512 + n * 256, 256)] = part[:, :256]
                 gwu[:, pl.ds(u * 512 + n * 256, 256)] = part[:, 256:]
 
-        units.append(unit(u, lambda q, u=u: gu_sum.at[u, :, q], gu_k.at[u], gu_1.at[u], gu_2.at[u], gu_3.at[u], gu_t.at[u], finish_gu))
+        units[f"G{u}"] = unit(u, lambda q, u=u: gu_sum.at[u, :, q], gu_k.at[u], gu_1.at[u], gu_2.at[u], gu_3.at[u], gu_t.at[u], finish_gu)
 
     def finish_o():
         low, high = halves(o_t)
         gwo[:, 0:384] = low
         gwo[:, 384:768] = high
 
-    units.append(unit(4, lambda q: o_sum.at[:, q], o_k, o_1, o_2, o_3, o_t, finish_o))
+    units["O"] = unit(4, lambda q: o_sum.at[:, q], o_k, o_1, o_2, o_3, o_t, finish_o)
 
     def finish_d():
         low, high = halves(d_t)
         gwd[:, 0:384] = low
         gwd[:, 384:768] = high
 
-    units.append(unit(5, lambda q: d_sum.at[:, q], d_k, d_1, d_2, d_3, d_t, finish_d))
+    units["D"] = unit(5, lambda q: d_sum.at[:, q], d_k, d_1, d_2, d_3, d_t, finish_d)
 
     q_swaps = [remote(gq_s.at[2 * m + 1 - pc.c], gq_r.at[m], qsend.at[m], qrecv.at[m], pc.other) for m in range(3)]
 
@@ -668,11 +705,9 @@
                 qk_k[m, :, i] = gq_r[m, :, q]
             q_swaps[m].wait_send()
 
-        units.append(unit(6 + m, lambda q, m=m: gq_r.at[m, :, q], qk_k.at[m], qk_1.at[m], qk_2.at[m], qk_3.at[m], qk_t.at[m], finish_q, source))
-    slots = fold(units)
-    ticks = {0: 0, 1: 1, 3: 2, 4: 3, 6: 4, 7: 5, 9: 6, 11: 7}
-
-    run_all(slots[0])
+        units[f"Q{m}"] = unit(6 + m, lambda q, m=m: gq_r.at[m, :, q], qk_k.at[m], qk_1.at[m], qk_2.at[m], qk_3.at[m], qk_t.at[m], finish_q, source)
+    ticks = Ticks(HIND, {f"{u}.r{k + 1}": step for u, steps in units.items() for k, step in enumerate(steps)})
+    ticks.at("enter")
     for copy in loads[:early]:
         copy.wait()
     ones = (lane_of(tok) < 3).astype(BF)
@@ -688,10 +723,7 @@
         kaug = jnp.concatenate([k_s[:, cs], seg_s[1]], axis=1)
         kt = k_s[:, cs].T
         for i in range(blocks):
-            if i in (1, 3):
-                for tick, slot in ticks.items():
-                    if slot and tick % 2 == i // 2:
-                        pl.when(j == tick // 2)(functools.partial(run_all, slots[slot]))
+            ticks.when(j, [f"A{t}.{i}" for t in range(6)])
             rs, first, last = pl.ds(i * 256, 256), i * 256, (i + 1) * 256
             qt, dt = q_s[rs, cs], do_s[rs, cs]
             prod = dt.astype(F32) * o_s[rs, cs].astype(F32)
@@ -734,6 +766,8 @@
         lax.fori_loop(0, blocks, finish, 0)
         pl.when(j == 0)(loads[early].wait)
 
+        ticks.when(j, [f"W{t}.0" for t in range(6)])
+
         def weight(z, carry):
             rows = nn(h1t_s[pl.ds(pl.multiple_of(z * 192, 64), 192), :], dqkv_s[:, pl.ds(pl.multiple_of(at, 128), 384)])
             gq_s[j, z] = rows.astype(BF).reshape(4, 48, 384)
@@ -745,13 +779,13 @@
         return carry
 
     lax.fori_loop(0, 6, pair, 0)
-    run_all(slots[8])
     for copy in loads[early + 1 :]:
         copy.wait()
     gg1_s[...] = jnp.zeros_like(gg1_s)
     gain1 = gain_ref[0:1, :]
 
     def last(r, carry):
+        ticks.when(r, [f"L.{i}" for i in range(4)])
         rs = pl.ds(pl.multiple_of(r * 256, 256), 256)
         dh1 = nt(dqkv_s[rs, :], flat(w_s[...]))
         x = x_s[rs, :].astype(F32)
@@ -760,8 +794,6 @@
         e1 = dh1 * gain1
         gg1_s[0:1, :] += jnp.sum(dh1 * n1, axis=0, keepdims=True)
         gx_ref[rs, :] = (dx2_s[rs, :] + r1 * (e1 - n1 * jnp.mean(e1 * n1, axis=1, keepdims=True))).astype(BF)
-        for t in range(4):
-            pl.when(r == t)(functools.partial(run_all, slots[9 + t]))
         return carry
 
     lax.fori_loop(0, blocks, last, 0)
@@ -782,6 +814,7 @@
         copy = remote(gg_st.at[to], gg_r.at[d - 1], gsend.at[d - 1], grecv.at[d - 1], {"wide": to})
         copy.start()
         copies.append(copy)
+    ticks.at("end")
     total = gg_st[pc.w]
     for d in range(1, 16):
         copies[d - 1].wait_recv()
@@ -789,10 +822,27 @@
     gg_c[0] = total
     to_core = remote(gg_c.at[0], gg_c.at[1], gsend.at[15], grecv.at[15], pc.other)
     to_core.start()
+    ticks.at("gains")
     to_core.wait()
     gg_out[...] = gg_c[0] + gg_c[1]
     for copy in copies:
         copy.wait_send()
+
+
+def tail_kernel(*refs):
+    gg_ref, stage, sem = refs[9], refs[21:30], refs[30]
+    into = [pltpu.make_async_copy(refs[k], stage[k], sem.at[0, k]) for k in range(9)]
+    out_of = [pltpu.make_async_copy(stage[k], refs[10 + k], sem.at[1, k]) for k in range(9)]
+    for copy in into:
+        copy.start()
+    for n in range(2):
+        out = refs[19 + n]
+        out[...] = jnp.sum(gg_ref[8 * n : 8 * n + 3, :], axis=0, keepdims=True)[:, : out.shape[1]]
+    for first, second in zip(into, out_of):
+        first.wait()
+        second.start()
+    for copy in out_of:
+        copy.wait()
 
 
 def shape(dims, dtype=BF):
@@ -804,32 +854,31 @@
     any_spec, vmem_spec = pl.BlockSpec(memory_space=pl.ANY), pl.BlockSpec(memory_space=pltpu.VMEM)
     dma = pltpu.SemaphoreType.DMA
     vm = pltpu.VMEM
-    tile = jnp.pad(jnp.stack([attn_gain, ffn_gain]), ((0, 14), (0, 128 - attn_gain.shape[0])))
     fore = pl.pallas_call(
         fore_kernel,
         out_shape=[
             shape((tok, width)), shape((tok, width)), shape((tok, width)), shape((tok, width)), shape((tok, width)),
             shape((width, tok)), shape((tok, 128), F32), shape((2, tok, 128)), shape((2, tok, 128), F32),
-            shape((4, 4, 48, 2304)), shape((tok, width), F32), shape((16, width), F32), shape((8, width), F32), shape((tok, width)),
+            shape((4, 4, 48, 2304)), shape((tok, width), F32), shape((8, width), F32), shape((8, width), F32), shape((tok, width)),
             shape((4, 4, 4, 48, 512)), shape((4, 4, 128, 384)), shape((4, 4, 48, 384)),
         ],
-        in_specs=[pl.BlockSpec(memory_space=pltpu.SMEM), vmem_spec, vmem_spec] + [any_spec] * 8,
+        in_specs=[pl.BlockSpec(memory_space=pltpu.SMEM)] + [vmem_spec] * 4 + [any_spec] * 7,
         out_specs=[any_spec] * 17,
         scratch_shapes=[
-            vm((4, 4, 48, 2304), BF), vm((4, 4, 48, 768), BF), vm((4, 4, 48, 4096), BF), vm((4, 4, 128, 768), BF), vm((16, 16, 128), BF), vm((16, width), F32),
+            vm((4, 4, 48, 2304), BF), vm((4, 4, 48, 768), BF), vm((4, 4, 48, 4096), BF), vm((4, 4, 128, 768), BF), vm((16, 8, 128), F32), vm((8, width), F32),
             vm((tok, width), F32), vm((tok, width), F32), vm((tok, width), F32), vm((width, tok), BF),
             vm((tok, width), BF), vm((tok, width), BF), vm((tok, width), BF), vm((tok, width), BF),
             vm((tok, 128), F32), vm((2, tok, 128), BF), vm((2, tok, 128), F32),
             vm((512, tok), BF), vm((tok, 1024), BF), vm((8, width), F32), vm((tok, width), BF),
             vm((2, 4, 4, 48, 1024), BF), vm((2, 4, 128, 768), BF), vm((4, 4, 48, 768), BF),
             vm((4, 4, 4, 48, 512), BF), vm((4, 4, 128, 384), BF), vm((4, 4, 48, 384), BF),
-            dma((31,)), dma((31,)), dma((7, 10)), dma((7, 10)), dma((15,)), dma((15,)), dma((9,)), dma((9,)), dma((20,)), dma((24,)),
+            dma((31,)), dma((31,)), dma((7, 10)), dma((7, 10)), dma((15,)), dma((15,)), dma((9,)), dma((9,)), dma((19,)), dma((24,)),
         ],
         compiler_params=pltpu.CompilerParams(collective_id=0, has_side_effects=True, vmem_limit_bytes=VMEM_BYTES),
         name="fore",
     )
     (q, k, v, o, do, h1t, lse, seg, rope, wqkv, dx2, gains, gg2, output, gu_sum, d_sum, o_sum) = fore(
-        seq_lengths, tokens, cotangent, tile, w_query, w_key, w_value, w_out, w_gate, w_up, w_down
+        seq_lengths, tokens, cotangent, attn_gain[None], ffn_gain[None], w_query, w_key, w_value, w_out, w_gate, w_up, w_down
     )
     hind = pl.pallas_call(
         hind_kernel,
@@ -853,7 +902,17 @@
     )
     gx, gwq, gwk, gwv, gwo, gwg, gwu, gwd, gg = hind(q, k, v, o, do, lse, seg, rope, h1t, wqkv, tokens, dx2, gains, gg2, gu_sum, d_sum, o_sum)
     count = attn_gain.shape[0]
-    return (output, gx, gwq, gwk, gwv, gwo, gwg, gwu, gwd, gg[0:3, :count].sum(axis=0), gg[8:11, :count].sum(axis=0))
+    large = (gwq, gwk, gwv, gwo, gwg, gwu, gwd, output, gx)
+    outs = pl.pallas_call(
+        tail_kernel,
+        out_shape=[shape(a.shape, a.dtype) for a in large] + [shape((1, count), F32)] * 2,
+        in_specs=[any_spec] * 9 + [vmem_spec],
+        out_specs=[any_spec] * 9 + [vmem_spec] * 2,
+        scratch_shapes=[vm(a.shape, a.dtype) for a in large] + [dma((2, 9))],
+        compiler_params=pltpu.CompilerParams(vmem_limit_bytes=VMEM_BYTES),
+        name="tail",
+    )(*large, gg)
+    return (outs[7], outs[8], *outs[:7], outs[9][0], outs[10][0])
 
 
 def layout(lengths, tok_count):

time: 246 us -> 216 us (0.88)
  Pallas kernels: 234 us -> 215 us
  local copies, waits for them, and re-layouts: 8.03 us -> 0 us
  other arithmetic: 2.48 us -> 0 us
    pallas_call x1, Pallas kernels: 98.7 us -> 87.7 us  [fast_body(): hind(q, k, v, o, do, lse, seg, rope, h1t, wqkv, tokens, dx2, gains, gg2,...]
    pallas_call x1 -> x2, Pallas kernels: 136 us -> 128 us  [the longest x1 122 us: fast_body(): fore(seq_lengths, tokens, cotangent, attn_gain[None], ffn_gain[None], w_q...]
    unnamed x27 -> x0, local copies, waits for them, and re-layouts: 8.03 us -> none
where the time goes in v2:
time: 216 us
  Pallas kernels  215 us (100%)
    pallas_call x1, Pallas kernels, fast_body(): fore(seq_lengths, tokens, cotangent, attn_gain[None], ffn_gain[None], w_q...  122 us
    pallas_call x1, Pallas kernels, fast_body(): hind(q, k, v, o, do, lse, seg, rope, h1t, wqkv, tokens, dx2, gains, gg2,...  87.7 us
    pallas_call x1, Pallas kernels, fast_body(): pl.pallas_call(tail_kernel, out_shape=[shape(a.shape, a.dtype) for a in l...  5.7 us

profile of v2, /device:TPU:0, one launch (start us, length us, event | category | flops | bytes accessed | tf_op | source)
XLA Modules:
  0.0 216.1 jit_solution(7601861905458580211)
XLA Ops:
  0.6 121.9 %fore.1 = (bf16[1024,768]{1,0:T(8,128)(2,1)}, bf16[1024,768]{1,0:T(8,128)(2,1)}, bf16[1024,768]{1,0:T(8,128)(2,1)}, bf16[1024,768]{1,0:T(8,128)(2,1)}, bf16[1024...) custom-call(s32[1,4]{1,0:T(1,128)} %lens.1, ...), custom_call_target="tpu_custom_call" | custom-call | tf_op jit(solution)/shard_map/fore/pallas_call | solution.py:880
  122.6 87.7 %hind.1 = (bf16[1024,768]{1,0:T(8,128)(2,1)}, f32[48,768]{1,0:T(8,128)}, f32[48,768]{1,0:T(8,128)}, f32[48,768]{1,0:T(8,128)}, f32[48,768]{1,0:T(8,128)}, /*inde...) custom-call(bf16[1024,768]{1,0:T(8,128)(2,1)} %get-tuple-element.48.q_hbm, ...), custom_call_target="tpu_custom_call" | custom-call | tf_op jit(solution)/shard_map/hind/pallas_call | solution.py:903
  210.2 5.7 %tail.1 = (f32[48,768]{1,0:T(8,128)}, f32[48,768]{1,0:T(8,128)}, f32[48,768]{1,0:T(8,128)}, f32[48,768]{1,0:T(8,128)}, f32[48,2048]{1,0:T(8,128)}, /*index=5*/f3...) custom-call(f32[48,768]{1,0:T(8,128)} %get-tuple-element.64.refs_0_,, ...), custom_call_target="tpu_custom_call" | custom-call | tf_op jit(solution)/shard_map/tail/pallas_call | solution.py:906

commit v3 on v2

--- a/solution.py
+++ b/solution.py
@@ -40,21 +40,79 @@
     return high, mid, (rest - mid.astype(F32)).astype(BF)
 
 
+ENTER, T, N, P_, A, M, F, B, W, L, END, GAINS = 0, 10, 20, 100, 200, 300, 400, 900, 910, 920, 930, 931
+Q0, Q1, Q2, O, D0, D1, G0, G1, G2, G3, D = range(0, 1100, 100)
 FORE = [
-    ("enter", "Q.s0"), ("Q1", "Q.a0 Q.b0"), ("Q2", "Q.p3 Q.b3 Q.a3 Q.p2"),
-    ("Q3", "Q.a2 D0.s0 Q.d3"), ("Q3", "Q.p1 Q.d0 Q.d2 O.s0"), ("Q3", "Q.b2 Q.a1 Q.b1 Q.d1"), ("Q3", "D0.s1 Q.s5"),
-    ("P.2", "O.s1"), ("P.3", "D1.s0"), ("A0.2", "O.s2"), ("A1.0", "G0.s0"), ("A1.3", "D1.s1"), ("A2.2", "G1.s0"), ("A2.3", "G0.s1"),
-    ("A3.1", "O.s3"), ("A3.2", "O.s4 D0.s2"), ("A4.0", "D1.s2 D0.s3"), ("A4.2", "G2.s0 G0.s2"), ("A5.1", "D0.s4"), ("A5.2", "G1.s1"),
-    ("A5.3", "D1.s3 O.s5"), ("M.0", "D0.s5 D1.s4"), ("M.0", "G0.s4 G0.s3"), ("M.2", "G2.s1 G3.s0"), ("F0.m0", "G0.s5 D1.s5 G1.s3"), ("F0.m2", "G1.s2"),
-    ("F0.g0", "G3.s1"), ("F0.g2", "G1.s4"), ("F0.g3", "G2.s2"), ("F1.m0", "G1.s5"), ("F1.g0", "G2.s4 G2.s3"), ("F1.g3", "G3.s2"), ("F1.d0", "G3.s3"),
-    ("F2.m0", "G2.s5"), ("F2.m3", "G3.s4"), ("F2.g3", "G3.s5"),
+    (ENTER, [Q0 + 0]),
+    (T + 1, [Q0 + 13]),
+    (T + 2, [Q0 + 12, Q0 + 20, Q0 + 11]),
+    (N + 0, [Q0 + 23]),
+    (N + 1, [Q0 + 22, Q0 + 40, Q1 + 0]),
+    (N + 2, [Q0 + 21, Q0 + 30, Q2 + 0, Q0 + 33]),
+    (N + 3, [Q0 + 31, Q0 + 43, Q0 + 42]),
+    (P_ + 0, [Q0 + 32, Q0 + 41, Q0 + 5]),
+    (P_ + 1, [Q1 + 1]),
+    (P_ + 3, [O + 0]),
+    (A + 2, [Q1 + 2]),
+    (A + 3, [Q2 + 1]),
+    (A + 10, [Q1 + 3]),
+    (A + 11, [D0 + 0, O + 1]),
+    (A + 12, [Q1 + 4, Q2 + 2]),
+    (P_ + 10, [Q1 + 5, Q2 + 3]),
+    (P_ + 11, [D1 + 0]),
+    (P_ + 12, [O + 2]),
+    (A + 21, [D0 + 1]),
+    (A + 22, [G0 + 0]),
+    (A + 30, [D1 + 1]),
+    (A + 31, [O + 4, Q2 + 4]),
+    (A + 32, [D0 + 2]),
+    (P_ + 20, [G0 + 1, Q2 + 5]),
+    (A + 40, [G1 + 0]),
+    (A + 43, [O + 3, D1 + 2, D0 + 3]),
+    (A + 50, [D1 + 3, G0 + 2, D0 + 4]),
+    (A + 51, [O + 5, G2 + 0]),
+    (A + 52, [G1 + 1]),
+    (A + 53, [G3 + 0]),
+    (M + 0, [G0 + 3]),
+    (M + 1, [D1 + 4]),
+    (M + 2, [D0 + 5]),
+    (M + 3, [G0 + 4, D1 + 5]),
+    (F + 0, [G1 + 2, G2 + 1, G0 + 5]),
+    (F + 10, [G3 + 1]),
+    (F + 11, [G1 + 3]),
+    (F + 12, [G1 + 4]),
+    (F + 13, [G2 + 2]),
+    (F + 100, [G1 + 5]),
+    (F + 101, [G2 + 3]),
+    (F + 102, [G3 + 2, G3 + 3]),
+    (F + 111, [G2 + 4]),
+    (F + 113, [G3 + 4]),
+    (F + 121, [G2 + 5]),
+    (F + 220, [G3 + 5]),
 ]
 HIND = [
-    ("enter", "G0.r1 G1.r1"), ("A0.3", "G0.r2 O.r1"), ("W0.0", "G1.r2"), ("A1.0", "D.r1"), ("A1.1", "G0.r3"), ("A1.3", "O.r2"), ("A2.0", "G1.r3 G2.r1"),
-    ("A3.1", "D.r2"), ("A3.2", "O.r3"), ("W3.0", "G2.r2 G3.r1"), ("A4.0", "Q0.r1 D.r3"), ("W4.0", "G2.r3"),
-    ("A5.1", "G3.r2 Q1.r1"), ("A5.2", "Q0.r2"), ("W5.0", "G3.r3"), ("L.0", "Q1.r2"), ("L.1", "Q0.r3"), ("L.2", "Q2.r1 Q1.r3"), ("L.3", "G1.r4"),
-    ("end", "G0.r4 D.r4 Q2.r2"), ("end", "O.r4 Q0.r4 O.r5 G2.r4"), ("end", "Q2.r3 D.r5 Q1.r4 G3.r4"), ("end", "G0.r5 G2.r5 G1.r5 Q0.r5"),
-    ("gains", "G3.r5 Q1.r5 Q2.r4 Q2.r5"),
+    (ENTER, [G0 + 1, G1 + 1]),
+    (A + 3, [G0 + 2, O + 1]),
+    (W + 0, [G1 + 2]),
+    (A + 10, [D + 1]),
+    (A + 11, [G0 + 3]),
+    (A + 13, [O + 2]),
+    (W + 1, [G1 + 3]),
+    (W + 1, [G2 + 1]),
+    (A + 31, [D + 2]),
+    (A + 32, [O + 3]),
+    (W + 3, [G2 + 2]),
+    (W + 3, [G3 + 1]),
+    (A + 40, [Q0 + 1, D + 3]),
+    (W + 4, [G2 + 3]),
+    (A + 51, [G3 + 2, Q1 + 1]),
+    (A + 52, [Q0 + 2]),
+    (W + 5, [G3 + 3]),
+    (L + 0, [Q1 + 2]),
+    (L + 1, [Q0 + 3]),
+    (L + 2, [Q2 + 1, Q1 + 3]),
+    (L + 3, [G1 + 4]),
+    (END, [G0 + 4, D + 4, Q2 + 2, O + 4, Q0 + 4, O + 5, G2 + 4, Q2 + 3, D + 5, Q1 + 4, G3 + 4, G0 + 5, G2 + 5, G1 + 5, Q0 + 5, G3 + 5, Q1 + 5, Q2 + 4, Q2 + 5]),
 ]
 
 
@@ -211,34 +269,30 @@
         for copy in [*zs, *first, *second, *onward, *sum(cores, [])]:
             copy.wait_send()
 
-    steps = {"s0": s0, "s5": s5}
-    for letter, step in (("p", p), ("a", a), ("b", b), ("d", c)):
+    steps = {0: s0, 5: s5}
+    for number, step in ((10, p), (20, a), (30, b), (40, c)):
         for d in range(4):
-            steps[f"{letter}{d}"] = functools.partial(step, d)
+            steps[number + d] = functools.partial(step, d)
+    del steps[10]
     return steps
-
-
-def pair_at(j):
-    return lax.rem(j, 2) * 1152 + (j // 2) * 384
 
 
 class Ticks:
     def __init__(self, table, steps):
         self.steps = steps
         self.table = {}
-        for name, listed in table:
-            self.table[name] = self.table.get(name, []) + listed.split()
-        asked = sum(self.table.values(), [])
-        assert sorted(asked) == sorted(steps), (set(asked) ^ set(steps))
-
-    def at(self, name):
-        for step in self.table.get(name, []):
+        for place, listed in table:
+            self.table[place] = self.table.get(place, []) + listed
+        assert sorted(sum(self.table.values(), [])) == sorted(steps)
+
+    def at(self, place):
+        for step in self.table.get(place, []):
             self.steps[step]()
 
-    def when(self, index, names):
-        for k, name in enumerate(names):
-            if name in self.table:
-                pl.when(index == k)(functools.partial(self.at, name))
+    def when(self, index, places):
+        for k, place in enumerate(places):
+            if place in self.table:
+                pl.when(index == k)(functools.partial(self.at, place))
 
 
 def turned(values, lane, back):
@@ -250,7 +304,7 @@
 
 def fore_kernel(
     lens, x_ref, dy_ref, g1_ref, g2_ref, wq, wk, wv, wo, wg, wu, wd,
-    q_out, k_out, v_out, o_out, do_out, h1t_out, lse_out, seg_out, rope_out, w_out, dx2_out, gain_out, gg_out, y_out, gu_sum, d_sum, o_sum,
+    q_out, k_out, v_out, o_out, do_out, h1t_out, lse_out, seg_out, rope_out, w_out, dx2_out, gain_out, gg_out, y_out, gu_sum, d_sum, o_sum, gu_first,
     w_s, wo_s, wgu_s, wd_s, gain_s, gains, x2_s, y_s, dh2_s, h1t_s, q_s, k_s, v_s, o_s, lse_s, seg_s, rope_s,
     hidt_s, dgu_s, gg_s, yb_s, gu_st, d_st, o_st, gu_r, d_r, o_r,
     wsend, wrecv, usend, urecv, gsend, grecv, rsend, rrecv, lsem, osem,
@@ -270,7 +324,7 @@
 
     for m in range(3):
         for n, w in enumerate((wq, wk, wv)):
-            load(w.at[:, half(m * 256, 128)], w_s.at[pc.z, pc.p, :, pl.ds(pl.multiple_of(pc.c * 1152 + m * 384 + n * 128, 128), 128)])
+            load(w.at[:, half(m * 256, 128)], w_s.at[m, pc.z, pc.p, :, pl.ds(pl.multiple_of(pc.c * 384 + n * 128, 128), 128)])
     early = len(loads)
     load(wo.at[:, half(0, 384)], wo_s.at[pc.z, pc.p, :, half(0, 384)])
     load(wd.at[:, half(0, 384)], wd_s.at[pc.z, pc.p, :, half(0, 384)])
@@ -312,32 +366,46 @@
         return carry
 
     units = {
-        "O": Gather(pc, wo_s, 0, 384, (0, 48), usend.at[0], urecv.at[0]),
-        "D0": Gather(pc, wd_s, 0, 384, (0, 64), usend.at[1], urecv.at[1]),
-        "D1": Gather(pc, wd_s, 0, 384, (64, 64), usend.at[2], urecv.at[2]),
+        Q1: Gather(pc, w_s.at[1], 0, 384, (0, 48), usend.at[7], urecv.at[7]),
+        Q2: Gather(pc, w_s.at[2], 0, 384, (0, 48), usend.at[8], urecv.at[8]),
+        O: Gather(pc, wo_s, 0, 384, (0, 48), usend.at[0], urecv.at[0]),
+        D0: Gather(pc, wd_s, 0, 384, (0, 64), usend.at[1], urecv.at[1]),
+        D1: Gather(pc, wd_s, 0, 384, (64, 64), usend.at[2], urecv.at[2]),
     }
     for u in range(4):
-        units[f"G{u}"] = Gather(pc, wgu_s, 1024 * u, 512, (0, 48), usend.at[3 + u], urecv.at[3 + u])
-    steps = {f"Q.{name}": step for name, step in piece_steps(Gather(pc, w_s, 0, 1152, (0, 48), wsend, wrecv)).items() if name != "p0"}
+        units[G0 + 100 * u] = Gather(pc, wgu_s, 1024 * u, 512, (0, 48), usend.at[3 + u], urecv.at[3 + u])
+    steps = {Q0 + k: step for k, step in piece_steps(Gather(pc, w_s.at[0], 0, 384, (0, 48), wsend, wrecv)).items()}
     for u, unit in units.items():
         for k, step in enumerate(block_steps(unit)):
-            steps[f"{u}.s{k}"] = step
+            steps[u + k] = step
     ticks = Ticks(FORE, steps)
-    ticks.at("enter")
+    ticks.at(ENTER)
     for copy in loads[early:]:
         copy.wait()
+    ticks.at(T)
     lax.fori_loop(0, blocks // 2, tables, 0)
-    ticks.at("Q1")
+    ticks.at(T + 1)
     lax.fori_loop(blocks // 2, blocks, tables, 0)
-    ticks.at("Q2")
     for copy in gain_copies:
         copy.wait_recv()
+    ticks.at(T + 2)
 
     def gain_rows(w, rows):
         return rows + nn(gain_s[w].astype(BF), spread(w))
 
     gains[...] = lax.fori_loop(0, 16, gain_rows, jnp.zeros((8, 768), F32))
-    ticks.at("Q3")
+    h1_s = yb_s
+
+    def norm(r, carry):
+        ticks.when(r, range(N, N + 4))
+        rs = pl.ds(pl.multiple_of(r * 256, 256), 256)
+        x = x_ref[rs, :].astype(F32)
+        h1 = (x * lax.rsqrt(jnp.mean(x * x, axis=1, keepdims=True) + EPS) * gains[0:1, :]).astype(BF)
+        h1_s[rs, :] = h1
+        h1t_s[:, rs] = h1.T
+        return carry
+
+    lax.fori_loop(0, blocks, norm, 0)
     outs = []
 
     def store(src, dst):
@@ -347,37 +415,32 @@
         return copy
 
     store(gains, gain_out)
-    store(w_s, w_out)
+    kept_h1t = store(h1t_s, h1t_out)
     store(seg_s, seg_out)
     store(rope_s, rope_out)
 
-    def project(r, carry):
-        ticks.when(r, [f"P.{i}" for i in range(4)])
-        rs = pl.ds(pl.multiple_of(r * 256, 256), 256)
-        lane = lane_of(256)
-        x = x_ref[rs, :].astype(F32)
-        h1 = (x * lax.rsqrt(jnp.mean(x * x, axis=1, keepdims=True) + EPS) * gains[0:1, :]).astype(BF)
-        h1t_s[:, rs] = h1.T
-        cos, sin = rope_s[0, rs, :], rope_s[1, rs, :]
-        for half in range(2):
-            pre = nn(h1, flat(w_s[:, :, :, half * 1152 : (half + 1) * 1152]))
-            for m in range(3):
-                cs = pl.ds((2 * m + half) * 128, 128)
-                qp, kp, vp = (pre[:, m * 384 + n * 128 : m * 384 + (n + 1) * 128] for n in range(3))
-                q_s[rs, cs] = ((qp * cos + turned(qp, lane, False) * sin).astype(BF).astype(F32) * 0.125).astype(BF)
+    def project(m, r, carry):
+        for k in range(2):
+            ticks.when(2 * m + r, [P_ + 10 * g + i for g in range(3) for i in (k, k + 2)])
+        for k in range(2):
+            rs = pl.ds(pl.multiple_of(r * 512 + k * 256, 256), 256)
+            lane = lane_of(256)
+            cos, sin = rope_s[0, rs, :], rope_s[1, rs, :]
+            pre = nn(h1_s[rs, :], flat(w_s[m]))
+            for n in range(2):
+                cs = pl.ds(pl.multiple_of((2 * m + n) * 128, 128), 128)
+                qp, kp, vp = (pre[:, n * 384 + t * 128 : n * 384 + (t + 1) * 128] for t in range(3))
+                q_s[rs, cs] = (qp * cos + turned(qp, lane, False) * sin).astype(BF) * BF(0.125)
                 k_s[rs, cs] = (kp * cos + turned(kp, lane, False) * sin).astype(BF)
                 v_s[rs, cs] = vp.astype(BF)
         return carry
-
-    lax.fori_loop(0, blocks, project, 0)
-    kept = [store(q_s, q_out), store(k_s, k_out), store(v_s, v_out), store(h1t_s, h1t_out)]
 
     def pair(j, carry):
         cs = pl.ds(pl.multiple_of(j * 128, 128), 128)
         lane = lane_of(256)
         below = lax.broadcasted_iota(jnp.int32, (256, 256), 0) >= lax.broadcasted_iota(jnp.int32, (256, 256), 1)
         for i in range(blocks):
-            ticks.when(j, [f"A{t}.{i}" for t in range(6)])
+            ticks.when(j, range(A + i, A + i + 60, 10))
             rs, before = pl.ds(i * 256, 256), pl.ds(0, i * 256)
             qt = q_s[rs, cs]
             parts = []
@@ -401,8 +464,15 @@
             o_s[rs, cs] = jnp.where(lane < 64, parts[0], parts[1]).astype(BF)
         return carry
 
+    def group(m, carry):
+        lax.fori_loop(0, blocks // 2, functools.partial(project, m), 0)
+        lax.fori_loop(2 * m, 2 * m + 2, pair, 0)
+        return carry
+
     lse_s[...] = jnp.zeros_like(lse_s)
-    lax.fori_loop(0, 6, pair, 0)
+    lax.fori_loop(0, 3, group, 0)
+    store(w_s, w_out)
+    kept = [store(q_s, q_out), store(k_s, k_out), store(v_s, v_out), kept_h1t]
     store(o_s, o_out)
     store(lse_s, lse_out)
     for copy in kept:
@@ -411,7 +481,7 @@
     gain2 = gains[1:2, :]
 
     def middle(r, carry):
-        ticks.when(r, [f"M.{i}" for i in range(4)])
+        ticks.when(r, range(M, M + 4))
         rs = pl.ds(pl.multiple_of(r * 256, 256), 256)
         x2 = x_ref[rs, :].astype(F32) + nn(o_s[rs, :], flat(wo_s[...]))
         x2_s[rs, :] = x2
@@ -431,6 +501,8 @@
 
     gu_swap = [swap(gu_st.at[u % 2], 512, gu_r.at[u], u) for u in range(4)]
     d_swap = [swap(d_st.at[u % 2], 384, d_r.at[u], 4 + u) for u in range(4)]
+
+    ahead = []
 
     def settle(u):
         gu_swap[u].wait_recv()
@@ -441,6 +513,11 @@
         mine = d_st[u % 2, :, :, pl.ds(pl.multiple_of(pc.c * 384, 128), 384)]
         d_r[u] = (d_r[u].astype(F32) + mine.astype(F32)).astype(BF)
         store(gu_r.at[u], gu_sum.at[u])
+        if u < 3:
+            for k, q in enumerate((pc.q1, pc.q3)):
+                copy = remote(gu_r.at[u, :, q], gu_first.at[u, :, k], rsend.at[9 + 2 * u + k], rrecv.at[9 + 2 * u + k], pc.first)
+                copy.start()
+                ahead.append(copy)
         store(d_r.at[u], d_sum.at[u])
         gu_swap[u].wait_send()
         d_swap[u].wait_send()
@@ -449,8 +526,9 @@
         wgu = pl.ds(u * 1024, 1024)
 
         def mix(r, carry):
-            ticks.when(r, [f"F{u}.m{i}" for i in range(4)])
-            rs = pl.ds(pl.multiple_of(r * 256, 256), 256)
+            for k in range(2):
+                ticks.when(r, range(F + 100 * u + k, F + 100 * u + 4, 2))
+            rs = pl.ds(pl.multiple_of(r * 512, 512), 512)
             both = nn(h2_s[rs, :], flat(wgu_s[:, :, :, wgu]))
             dhid = nt(dy_ref[rs, :], flat(wd_s[u]))
             hids, grads = [], []
@@ -476,12 +554,12 @@
                 dh2_s[rs, :] += dv
             return carry
 
-        lax.fori_loop(0, blocks, mix, 0)
+        lax.fori_loop(0, blocks // 2, mix, 0)
         if u >= 2:
             settle(u - 2)
 
         def weight_gu(z, carry):
-            ticks.when(z, [f"F{u}.g{i}" for i in range(4)])
+            ticks.when(z, range(F + 100 * u + 10, F + 100 * u + 14))
             rows = nn(h2t_s[pl.ds(pl.multiple_of(z * 192, 64), 192), :], dgu_s[...])
             gu_st[u % 2, z] = rows.astype(BF).reshape(4, 48, 1024)
             return carry
@@ -489,7 +567,7 @@
         lax.fori_loop(0, 4, weight_gu, 0)
 
         def weight_d(k, carry):
-            ticks.when(k, [f"F{u}.d{i}" for i in range(2)])
+            ticks.when(k, range(F + 100 * u + 20, F + 100 * u + 22))
             rows = nn(hidt_s[pl.ds(pl.multiple_of(k * 256, 256), 256), :], dy_ref[...])
             d_st[u % 2, pl.ds(k * 2, 2)] = rows.astype(BF).reshape(2, 128, 768)
             return carry
@@ -498,6 +576,7 @@
         gu_swap[u].start()
         d_swap[u].start()
 
+    settle(2)
     gg_s[...] = jnp.zeros_like(gg_s)
 
     def back(r, carry):
@@ -510,18 +589,15 @@
         gg_s[0:1, :] += jnp.sum(dh2 * n2, axis=0, keepdims=True)
         dx2 = dy_ref[rs, :].astype(F32) + r2 * (e2 - n2 * jnp.mean(e2 * n2, axis=1, keepdims=True))
         x2_s[rs, :] = dx2
-        dxb = dx2.astype(BF)
-        dxb_s[rs, :] = dxb
-        do_s[rs, :] = nt(dxb, flat(wo_s[...])).astype(BF)
+        dxb_s[rs, :] = dx2.astype(BF)
         h2t_s[:, rs] = o_s[rs, :].T
         return carry
 
     lax.fori_loop(0, blocks, back, 0)
     store(yb_s, y_out)
     store(x2_s, dx2_out)
-    store(do_s, do_out)
     store(gg_s, gg_out)
-    settle(2)
+    settle(3)
 
     def weight_o(z, carry):
         rows = nn(h2t_s[pl.ds(pl.multiple_of(z * 192, 64), 192), :], dxb_s[...])
@@ -531,12 +607,21 @@
     lax.fori_loop(0, 4, weight_o, 0)
     o_swap = swap(o_st, 384, o_r, 8)
     o_swap.start()
-    settle(3)
+
+    def back_out(r, carry):
+        rs = pl.ds(pl.multiple_of(r * 256, 256), 256)
+        do_s[rs, :] = nt(dxb_s[rs, :], flat(wo_s[...])).astype(BF)
+        return carry
+
+    lax.fori_loop(0, blocks, back_out, 0)
+    store(do_s, do_out)
     o_swap.wait_recv()
     mine = o_st[:, :, :, pl.ds(pl.multiple_of(pc.c * 384, 128), 384)]
     o_r[...] = (o_r[...].astype(F32) + mine.astype(F32)).astype(BF)
     store(o_r, o_sum)
     o_swap.wait_send()
+    for copy in ahead:
+        copy.wait()
     for copy in gain_copies:
         copy.wait_send()
     for copy in outs:
@@ -548,7 +633,9 @@
     def __init__(self, place, keep, r1, r2, r3, total, other_total, send, recv, far1, far2, near):
         pc = place
         self.pc, self.keep, self.r1, self.r2, self.r3, self.total = pc, keep, r1, r2, r3, total
-        self.to_first = [remote(ref, r1.at[:, i], send.at[i], recv.at[i], pc.first) for i, ref in enumerate((far1, far2))]
+        self.to_first = []
+        if far1 is not None:
+            self.to_first = [remote(ref, r1.at[:, i], send.at[i], recv.at[i], pc.first) for i, ref in enumerate((far1, far2))]
         self.near = near
         self.to_second = remote(keep.at[:, 1], r2, send.at[2], recv.at[2], pc.second)
         self.zs = [remote(keep.at[pc.z_at(d), 0], r3.at[d - 1], send.at[2 + d], recv.at[2 + d], pc.z_dev(d)) for d in (1, 2, 3)]
@@ -605,7 +692,7 @@
 
 
 def hind_kernel(
-    q_hbm, k_hbm, v_hbm, o_hbm, do_hbm, lse_hbm, seg_hbm, rope_hbm, h1t_hbm, w_hbm, x_hbm, dx2_hbm, gain_ref, gg_ref, gu_sum, d_sum, o_sum,
+    q_hbm, k_hbm, v_hbm, o_hbm, do_hbm, lse_hbm, seg_hbm, rope_hbm, h1t_hbm, w_hbm, x_hbm, dx2_hbm, gain_ref, gg_ref, gu_sum, d_sum, o_sum, gu_first,
     gx_ref, gwq, gwk, gwv, gwo, gwg, gwu, gwd, gg_out,
     q_s, k_s, v_s, o_s, do_s, lse_s, seg_s, rope_s, h1t_s, w_s, x_s, dx2_s, dqkv_s, dk_s, dv_s,
     gq_s, gq_r, gu_k, gu_1, gu_2, gu_3, gu_t, d_k, d_1, d_2, d_3, d_t, o_k, o_1, o_2, o_3, o_t, qk_k, qk_1, qk_2, qk_3, qk_t,
@@ -636,11 +723,15 @@
         for copy in copies:
             copy.start()
 
-    def unit(n, parts, keep, r1, r2, r3, total, finish, source=None):
+    def unit(n, parts, keep, r1, r2, r3, total, finish, source=None, done=None):
         near = []
         if source is None:
             near = [pltpu.make_async_copy(parts(q), keep.at[:, i], nsem.at[n, i]) for i, q in enumerate((pc.p, pc.q2))]
-        red = Reduce(pc, keep, r1, r2, r3, total.at[0], total.at[1], ssend.at[n], srecv.at[n], parts(pc.q1), parts(pc.q3), near)
+        far = (parts(pc.q1), parts(pc.q3))
+        if done is not None:
+            near.append(pltpu.make_async_copy(done, r1, nsem.at[n, 2]))
+            far = (None, None)
+        red = Reduce(pc, keep, r1, r2, r3, total.at[0], total.at[1], ssend.at[n], srecv.at[n], *far, near)
 
         def begin():
             if source is not None:
@@ -663,21 +754,22 @@
                 gwg[:, pl.ds(u * 512 + n * 256, 256)] = part[:, :256]
                 gwu[:, pl.ds(u * 512 + n * 256, 256)] = part[:, 256:]
 
-        units[f"G{u}"] = unit(u, lambda q, u=u: gu_sum.at[u, :, q], gu_k.at[u], gu_1.at[u], gu_2.at[u], gu_3.at[u], gu_t.at[u], finish_gu)
+        done = gu_first.at[u] if u < 3 else None
+        units[G0 + 100 * u] = unit(u, lambda q, u=u: gu_sum.at[u, :, q], gu_k.at[u], gu_1.at[u], gu_2.at[u], gu_3.at[u], gu_t.at[u], finish_gu, done=done)
 
     def finish_o():
         low, high = halves(o_t)
         gwo[:, 0:384] = low
         gwo[:, 384:768] = high
 
-    units["O"] = unit(4, lambda q: o_sum.at[:, q], o_k, o_1, o_2, o_3, o_t, finish_o)
+    units[O] = unit(4, lambda q: o_sum.at[:, q], o_k, o_1, o_2, o_3, o_t, finish_o)
 
     def finish_d():
         low, high = halves(d_t)
         gwd[:, 0:384] = low
         gwd[:, 384:768] = high
 
-    units["D"] = unit(5, lambda q: d_sum.at[:, q], d_k, d_1, d_2, d_3, d_t, finish_d)
+    units[D] = unit(5, lambda q: d_sum.at[:, q], d_k, d_1, d_2, d_3, d_t, finish_d)
 
     q_swaps = [remote(gq_s.at[2 * m + 1 - pc.c], gq_r.at[m], qsend.at[m], qrecv.at[m], pc.other) for m in range(3)]
 
@@ -705,9 +797,9 @@
                 qk_k[m, :, i] = gq_r[m, :, q]
             q_swaps[m].wait_send()
 
-        units[f"Q{m}"] = unit(6 + m, lambda q, m=m: gq_r.at[m, :, q], qk_k.at[m], qk_1.at[m], qk_2.at[m], qk_3.at[m], qk_t.at[m], finish_q, source)
-    ticks = Ticks(HIND, {f"{u}.r{k + 1}": step for u, steps in units.items() for k, step in enumerate(steps)})
-    ticks.at("enter")
+        units[Q0 + 100 * m] = unit(6 + m, lambda q, m=m: gq_r.at[m, :, q], qk_k.at[m], qk_1.at[m], qk_2.at[m], qk_3.at[m], qk_t.at[m], finish_q, source)
+    ticks = Ticks(HIND, {u + k + 1: step for u, steps in units.items() for k, step in enumerate(steps)})
+    ticks.at(ENTER)
     for copy in loads[:early]:
         copy.wait()
     ones = (lane_of(tok) < 3).astype(BF)
@@ -716,14 +808,14 @@
         cs = pl.ds(pl.multiple_of(j * 128, 128), 128)
         lane = lane_of(256)
         above = lax.broadcasted_iota(jnp.int32, (256, 256), 0) <= lax.broadcasted_iota(jnp.int32, (256, 256), 1)
-        at = pair_at(j)
+        at = j * 384
         dk_s[...] = jnp.zeros_like(dk_s)
         dv_s[...] = jnp.zeros_like(dv_s)
         vaug = jnp.concatenate([v_s[:, cs], ones], axis=1)
         kaug = jnp.concatenate([k_s[:, cs], seg_s[1]], axis=1)
         kt = k_s[:, cs].T
         for i in range(blocks):
-            ticks.when(j, [f"A{t}.{i}" for t in range(6)])
+            ticks.when(j, range(A + i, A + i + 60, 10))
             rs, first, last = pl.ds(i * 256, 256), i * 256, (i + 1) * 256
             qt, dt = q_s[rs, cs], do_s[rs, cs]
             prod = dt.astype(F32) * o_s[rs, cs].astype(F32)
@@ -766,7 +858,7 @@
         lax.fori_loop(0, blocks, finish, 0)
         pl.when(j == 0)(loads[early].wait)
 
-        ticks.when(j, [f"W{t}.0" for t in range(6)])
+        ticks.when(j, range(W, W + 6))
 
         def weight(z, carry):
             rows = nn(h1t_s[pl.ds(pl.multiple_of(z * 192, 64), 192), :], dqkv_s[:, pl.ds(pl.multiple_of(at, 128), 384)])
@@ -785,36 +877,28 @@
     gain1 = gain_ref[0:1, :]
 
     def last(r, carry):
-        ticks.when(r, [f"L.{i}" for i in range(4)])
+        ticks.when(r, range(L, L + 4))
         rs = pl.ds(pl.multiple_of(r * 256, 256), 256)
-        dh1 = nt(dqkv_s[rs, :], flat(w_s[...]))
+        dh1 = sum(nt(dqkv_s[rs, m * 768 : (m + 1) * 768], flat(w_s[m])) for m in range(3))
         x = x_s[rs, :].astype(F32)
         r1 = lax.rsqrt(jnp.mean(x * x, axis=1, keepdims=True) + EPS)
         n1 = x * r1
         e1 = dh1 * gain1
-        gg1_s[0:1, :] += jnp.sum(dh1 * n1, axis=0, keepdims=True)
+        gg1_s[0:1, 0:768] += jnp.sum(dh1 * n1, axis=0, keepdims=True)
         gx_ref[rs, :] = (dx2_s[rs, :] + r1 * (e1 - n1 * jnp.mean(e1 * n1, axis=1, keepdims=True))).astype(BF)
         return carry
 
     lax.fori_loop(0, blocks, last, 0)
-    row = lax.broadcasted_iota(jnp.int32, (16, 768), 0)
-    terms = jnp.zeros((16, 768), BF)
-    for n, sums in enumerate((gg1_s, gg_ref)):
-        for k, term in enumerate(three_way(sums[0:1, :])):
-            terms = jnp.where(row == 8 * n + k, term, terms)
-
-    def cut(w, carry):
-        gg_st[w] = nt(terms, spread(w))
-        return carry
-
-    lax.fori_loop(0, 16, cut, 0)
+    gg1_s[1:2, 0:768] = gg_ref[0:1, :]
+    for w in range(16):
+        gg_st[w] = gg1_s[:, 48 * w : 48 * w + 128]
     copies = []
     for d in range(1, 16):
         to = lax.rem(pc.w + d, 16)
         copy = remote(gg_st.at[to], gg_r.at[d - 1], gsend.at[d - 1], grecv.at[d - 1], {"wide": to})
         copy.start()
         copies.append(copy)
-    ticks.at("end")
+    ticks.at(END)
     total = gg_st[pc.w]
     for d in range(1, 16):
         copies[d - 1].wait_recv()
@@ -822,7 +906,7 @@
     gg_c[0] = total
     to_core = remote(gg_c.at[0], gg_c.at[1], gsend.at[15], grecv.at[15], pc.other)
     to_core.start()
-    ticks.at("gains")
+    ticks.at(GAINS)
     to_core.wait()
     gg_out[...] = gg_c[0] + gg_c[1]
     for copy in copies:
@@ -837,7 +921,7 @@
         copy.start()
     for n in range(2):
         out = refs[19 + n]
-        out[...] = jnp.sum(gg_ref[8 * n : 8 * n + 3, :], axis=0, keepdims=True)[:, : out.shape[1]]
+        out[...] = gg_ref[n : n + 1, : out.shape[1]]
     for first, second in zip(into, out_of):
         first.wait()
         second.start()
@@ -859,48 +943,48 @@
         out_shape=[
             shape((tok, width)), shape((tok, width)), shape((tok, width)), shape((tok, width)), shape((tok, width)),
             shape((width, tok)), shape((tok, 128), F32), shape((2, tok, 128)), shape((2, tok, 128), F32),
-            shape((4, 4, 48, 2304)), shape((tok, width), F32), shape((8, width), F32), shape((8, width), F32), shape((tok, width)),
-            shape((4, 4, 4, 48, 512)), shape((4, 4, 128, 384)), shape((4, 4, 48, 384)),
+            shape((3, 4, 4, 48, 768)), shape((tok, width), F32), shape((8, width), F32), shape((8, width), F32), shape((tok, width)),
+            shape((4, 4, 4, 48, 512)), shape((4, 4, 128, 384)), shape((4, 4, 48, 384)), shape((3, 4, 2, 48, 512)),
         ],
         in_specs=[pl.BlockSpec(memory_space=pltpu.SMEM)] + [vmem_spec] * 4 + [any_spec] * 7,
-        out_specs=[any_spec] * 17,
+        out_specs=[any_spec] * 18,
         scratch_shapes=[
-            vm((4, 4, 48, 2304), BF), vm((4, 4, 48, 768), BF), vm((4, 4, 48, 4096), BF), vm((4, 4, 128, 768), BF), vm((16, 8, 128), F32), vm((8, width), F32),
+            vm((3, 4, 4, 48, 768), BF), vm((4, 4, 48, 768), BF), vm((4, 4, 48, 4096), BF), vm((4, 4, 128, 768), BF), vm((16, 8, 128), F32), vm((8, width), F32),
             vm((tok, width), F32), vm((tok, width), F32), vm((tok, width), F32), vm((width, tok), BF),
             vm((tok, width), BF), vm((tok, width), BF), vm((tok, width), BF), vm((tok, width), BF),
             vm((tok, 128), F32), vm((2, tok, 128), BF), vm((2, tok, 128), F32),
             vm((512, tok), BF), vm((tok, 1024), BF), vm((8, width), F32), vm((tok, width), BF),
             vm((2, 4, 4, 48, 1024), BF), vm((2, 4, 128, 768), BF), vm((4, 4, 48, 768), BF),
             vm((4, 4, 4, 48, 512), BF), vm((4, 4, 128, 384), BF), vm((4, 4, 48, 384), BF),
-            dma((31,)), dma((31,)), dma((7, 10)), dma((7, 10)), dma((15,)), dma((15,)), dma((9,)), dma((9,)), dma((19,)), dma((24,)),
+            dma((31,)), dma((31,)), dma((9, 10)), dma((9, 10)), dma((15,)), dma((15,)), dma((15,)), dma((15,)), dma((19,)), dma((24,)),
         ],
         compiler_params=pltpu.CompilerParams(collective_id=0, has_side_effects=True, vmem_limit_bytes=VMEM_BYTES),
         name="fore",
     )
-    (q, k, v, o, do, h1t, lse, seg, rope, wqkv, dx2, gains, gg2, output, gu_sum, d_sum, o_sum) = fore(
+    (q, k, v, o, do, h1t, lse, seg, rope, wqkv, dx2, gains, gg2, output, gu_sum, d_sum, o_sum, gu_first) = fore(
         seq_lengths, tokens, cotangent, attn_gain[None], ffn_gain[None], w_query, w_key, w_value, w_out, w_gate, w_up, w_down
     )
     hind = pl.pallas_call(
         hind_kernel,
-        out_shape=[shape((tok, width))] + [shape((48, width), F32)] * 4 + [shape((48, 2048), F32)] * 2 + [shape((128, width), F32), shape((16, 128), F32)],
-        in_specs=[any_spec] * 12 + [vmem_spec] * 2 + [any_spec] * 3,
+        out_shape=[shape((tok, width))] + [shape((48, width), F32)] * 4 + [shape((48, 2048), F32)] * 2 + [shape((128, width), F32), shape((8, 128), F32)],
+        in_specs=[any_spec] * 12 + [vmem_spec] * 2 + [any_spec] * 4,
         out_specs=[vmem_spec] * 9,
         scratch_shapes=[
             vm((tok, width), BF), vm((tok, width), BF), vm((tok, width), BF), vm((tok, width), BF), vm((tok, width), BF),
-            vm((tok, 128), F32), vm((2, tok, 128), BF), vm((2, tok, 128), F32), vm((width, tok), BF), vm((4, 4, 48, 2304), BF),
+            vm((tok, 128), F32), vm((2, tok, 128), BF), vm((2, tok, 128), F32), vm((width, tok), BF), vm((3, 4, 4, 48, 768), BF),
             vm((tok, width), BF), vm((tok, width), F32), vm((tok, 2304), BF), vm((tok, 128), F32), vm((tok, 128), F32),
             vm((6, 4, 4, 48, 384), BF), vm((3, 4, 4, 48, 384), BF),
             vm((4, 4, 2, 48, 512), BF), vm((4, 4, 2, 48, 512), BF), vm((4, 4, 48, 512), BF), vm((4, 3, 48, 512), BF), vm((4, 2, 48, 512), F32),
             vm((4, 2, 128, 384), BF), vm((4, 2, 128, 384), BF), vm((4, 128, 384), BF), vm((3, 128, 384), BF), vm((2, 128, 384), F32),
             vm((4, 2, 48, 384), BF), vm((4, 2, 48, 384), BF), vm((4, 48, 384), BF), vm((3, 48, 384), BF), vm((2, 48, 384), F32),
             vm((3, 4, 2, 48, 384), BF), vm((3, 4, 2, 48, 384), BF), vm((3, 4, 48, 384), BF), vm((3, 3, 48, 384), BF), vm((3, 2, 48, 384), F32),
-            vm((8, width), F32), vm((16, 16, 128), F32), vm((15, 16, 128), F32), vm((2, 16, 128), F32),
-            dma((12,)), dma((6, 2)), dma((9, 7)), dma((9, 7)), dma((3,)), dma((3,)), dma((16,)), dma((16,)),
+            vm((8, width + 128), F32), vm((16, 8, 128), F32), vm((15, 8, 128), F32), vm((2, 8, 128), F32),
+            dma((12,)), dma((6, 3)), dma((9, 7)), dma((9, 7)), dma((3,)), dma((3,)), dma((16,)), dma((16,)),
         ],
         compiler_params=pltpu.CompilerParams(collective_id=1, has_side_effects=True, vmem_limit_bytes=VMEM_BYTES),
         name="hind",
     )
-    gx, gwq, gwk, gwv, gwo, gwg, gwu, gwd, gg = hind(q, k, v, o, do, lse, seg, rope, h1t, wqkv, tokens, dx2, gains, gg2, gu_sum, d_sum, o_sum)
+    gx, gwq, gwk, gwv, gwo, gwg, gwu, gwd, gg = hind(q, k, v, o, do, lse, seg, rope, h1t, wqkv, tokens, dx2, gains, gg2, gu_sum, d_sum, o_sum, gu_first)
     count = attn_gain.shape[0]
     large = (gwq, gwk, gwv, gwo, gwg, gwu, gwd, output, gx)
     outs = pl.pallas_call(

time: 216 us -> 204 us (0.944)
  Pallas kernels: 215 us -> 203 us
    pallas_call x1, Pallas kernels: 122 us -> 116 us  [fast_body(): fore(seq_lengths, tokens, cotangent, attn_gain[None], ffn_gain[None], w_q...]
    pallas_call x1, Pallas kernels: 87.7 us -> 82.1 us  [fast_body(): hind(q, k, v, o, do, lse, seg, rope, h1t, wqkv, tokens, dx2, gains, gg2,...]
where the time goes in v3:
time: 204 us
  Pallas kernels  203 us (100%)
    pallas_call x1, Pallas kernels, fast_body(): fore(seq_lengths, tokens, cotangent, attn_gain[None], ffn_gain[None], w_q...  116 us
    pallas_call x1, Pallas kernels, fast_body(): hind(q, k, v, o, do, lse, seg, rope, h1t, wqkv, tokens, dx2, gains, gg2,...  82.1 us
    pallas_call x1, Pallas kernels, fast_body(): pl.pallas_call(tail_kernel, out_shape=[shape(a.shape, a.dtype) for a in l...  5.68 us

profile of v3, /device:TPU:0, one launch (start us, length us, event | category | flops | bytes accessed | tf_op | source)
XLA Modules:
  0.0 204.2 jit_solution(9890806266970475004)
XLA Ops:
  0.6 115.6 %fore.1 = (bf16[1024,768]{1,0:T(8,128)(2,1)}, bf16[1024,768]{1,0:T(8,128)(2,1)}, bf16[1024,768]{1,0:T(8,128)(2,1)}, bf16[1024,768]{1,0:T(8,128)(2,1)}, bf16[1024...) custom-call(s32[1,4]{1,0:T(1,128)} %lens.1, ...), custom_call_target="tpu_custom_call" | custom-call | tf_op jit(solution)/shard_map/fore/pallas_call | solution.py:964
  116.2 82.1 %hind.1 = (bf16[1024,768]{1,0:T(8,128)(2,1)}, f32[48,768]{1,0:T(8,128)}, f32[48,768]{1,0:T(8,128)}, f32[48,768]{1,0:T(8,128)}, f32[48,768]{1,0:T(8,128)}, /*inde...) custom-call(bf16[1024,768]{1,0:T(8,128)(2,1)} %get-tuple-element.49.q_hbm, ...), custom_call_target="tpu_custom_call" | custom-call | tf_op jit(solution)/shard_map/hind/pallas_call | solution.py:987
  198.4 5.7 %tail.1 = (f32[48,768]{1,0:T(8,128)}, f32[48,768]{1,0:T(8,128)}, f32[48,768]{1,0:T(8,128)}, f32[48,768]{1,0:T(8,128)}, f32[48,2048]{1,0:T(8,128)}, /*index=5*/f3...) custom-call(f32[48,768]{1,0:T(8,128)} %get-tuple-element.66.refs_0_,, ...), custom_call_target="tpu_custom_call" | custom-call | tf_op jit(solution)/shard_map/tail/pallas_call | solution.py:990

commit v4 on v3

--- a/solution.py
+++ b/solution.py
@@ -438,30 +438,29 @@
     def pair(j, carry):
         cs = pl.ds(pl.multiple_of(j * 128, 128), 128)
         lane = lane_of(256)
-        below = lax.broadcasted_iota(jnp.int32, (256, 256), 0) >= lax.broadcasted_iota(jnp.int32, (256, 256), 1)
+        row = lax.broadcasted_iota(jnp.int32, (512, 256), 0)
+        below = jnp.where(row >= 256, row - 256, row) >= lax.broadcasted_iota(jnp.int32, (512, 256), 1)
         for i in range(blocks):
             ticks.when(j, range(A + i, A + i + 60, 10))
             rs, before = pl.ds(i * 256, 256), pl.ds(0, i * 256)
-            qt = q_s[rs, cs]
-            parts = []
-            for h in range(2):
-                qm = jnp.where((lane < 64) == (h == 0), qt, BF(0))
-                qm = jnp.concatenate([qm, seg_s[0, rs, :]], axis=1)
-                sd = jnp.where(below, nt(qm, jnp.concatenate([k_s[rs, cs], seg_s[1, rs, :]], axis=1)), NEG)
-                top = jnp.max(sd, axis=1, keepdims=True)
-                if i:
-                    so = nt(qm, jnp.concatenate([k_s[before, cs], seg_s[1, before, :]], axis=1))
-                    top = jnp.maximum(top, jnp.max(so, axis=1, keepdims=True))
-                pd = jnp.exp(sd - top)
-                mass = jnp.sum(pd, axis=1, keepdims=True)
-                acc = nn(pd.astype(BF), v_s[rs, cs])
-                if i:
-                    po = jnp.exp(so - top)
-                    mass = mass + jnp.sum(po, axis=1, keepdims=True)
-                    acc = acc + nn(po.astype(BF), v_s[before, cs])
-                parts.append(acc * (1.0 / mass))
-                lse_s[rs, :] = jnp.where(lane == 2 * j + h, top + jnp.log(mass), lse_s[rs, :])
-            o_s[rs, cs] = jnp.where(lane < 64, parts[0], parts[1]).astype(BF)
+            qt, seg = q_s[rs, cs], seg_s[0, rs, :]
+            qm = jnp.concatenate([jnp.concatenate([jnp.where((lane < 64) == (h == 0), qt, BF(0)), seg], axis=1) for h in range(2)], axis=0)
+            sd = jnp.where(below, nt(qm, jnp.concatenate([k_s[rs, cs], seg_s[1, rs, :]], axis=1)), NEG)
+            top = jnp.max(sd, axis=1, keepdims=True)
+            if i:
+                so = nt(qm, jnp.concatenate([k_s[before, cs], seg_s[1, before, :]], axis=1))
+                top = jnp.maximum(top, jnp.max(so, axis=1, keepdims=True))
+            pd = jnp.exp(sd - top)
+            mass = jnp.sum(pd, axis=1, keepdims=True)
+            acc = nn(pd.astype(BF), v_s[rs, cs])
+            if i:
+                po = jnp.exp(so - top)
+                mass = mass + jnp.sum(po, axis=1, keepdims=True)
+                acc = acc + nn(po.astype(BF), v_s[before, cs])
+            acc = acc * (1.0 / mass)
+            lse = top + jnp.log(mass)
+            lse_s[rs, :] = jnp.where(lane == 2 * j, lse[:256], jnp.where(lane == 2 * j + 1, lse[256:], lse_s[rs, :]))
+            o_s[rs, cs] = jnp.where(lane < 64, acc[:256], acc[256:]).astype(BF)
         return carry
 
     def group(m, carry):
@@ -481,8 +480,9 @@
     gain2 = gains[1:2, :]
 
     def middle(r, carry):
-        ticks.when(r, range(M, M + 4))
-        rs = pl.ds(pl.multiple_of(r * 256, 256), 256)
+        for k in range(2):
+            ticks.when(r, range(M + k, M + 4, 2))
+        rs = pl.ds(pl.multiple_of(r * 512, 512), 512)
         x2 = x_ref[rs, :].astype(F32) + nn(o_s[rs, :], flat(wo_s[...]))
         x2_s[rs, :] = x2
         h2 = (x2 * lax.rsqrt(jnp.mean(x2 * x2, axis=1, keepdims=True) + EPS) * gain2).astype(BF)
@@ -490,7 +490,7 @@
         h2t_s[:, rs] = h2.T
         return carry
 
-    lax.fori_loop(0, blocks, middle, 0)
+    lax.fori_loop(0, blocks // 2, middle, 0)
 
     def swap(buf, width, got, k):
         far = pl.ds(pl.multiple_of((1 - pc.c) * width, 128), width)
@@ -559,20 +559,17 @@
             settle(u - 2)
 
         def weight_gu(z, carry):
-            ticks.when(z, range(F + 100 * u + 10, F + 100 * u + 14))
-            rows = nn(h2t_s[pl.ds(pl.multiple_of(z * 192, 64), 192), :], dgu_s[...])
-            gu_st[u % 2, z] = rows.astype(BF).reshape(4, 48, 1024)
+            for k in range(2):
+                ticks.when(z, range(F + 100 * u + 10 + k, F + 100 * u + 14, 2))
+            rows = nn(h2t_s[pl.ds(pl.multiple_of(z * 384, 128), 384), :], dgu_s[...])
+            gu_st[u % 2, pl.ds(2 * z, 2)] = rows.astype(BF).reshape(2, 4, 48, 1024)
             return carry
 
-        lax.fori_loop(0, 4, weight_gu, 0)
-
-        def weight_d(k, carry):
-            ticks.when(k, range(F + 100 * u + 20, F + 100 * u + 22))
-            rows = nn(hidt_s[pl.ds(pl.multiple_of(k * 256, 256), 256), :], dy_ref[...])
-            d_st[u % 2, pl.ds(k * 2, 2)] = rows.astype(BF).reshape(2, 128, 768)
-            return carry
-
-        lax.fori_loop(0, 2, weight_d, 0)
+        lax.fori_loop(0, 2, weight_gu, 0)
+
+        for k in range(2):
+            ticks.at(F + 100 * u + 20 + k)
+        d_st[u % 2] = nn(hidt_s[...], dy_ref[...]).astype(BF).reshape(4, 128, 768)
         gu_swap[u].start()
         d_swap[u].start()
 
@@ -600,20 +597,20 @@
     settle(3)
 
     def weight_o(z, carry):
-        rows = nn(h2t_s[pl.ds(pl.multiple_of(z * 192, 64), 192), :], dxb_s[...])
-        o_st[z] = rows.astype(BF).reshape(4, 48, 768)
+        rows = nn(h2t_s[pl.ds(pl.multiple_of(z * 384, 128), 384), :], dxb_s[...])
+        o_st[pl.ds(2 * z, 2)] = rows.astype(BF).reshape(2, 4, 48, 768)
         return carry
 
-    lax.fori_loop(0, 4, weight_o, 0)
+    lax.fori_loop(0, 2, weight_o, 0)
     o_swap = swap(o_st, 384, o_r, 8)
     o_swap.start()
 
     def back_out(r, carry):
-        rs = pl.ds(pl.multiple_of(r * 256, 256), 256)
+        rs = pl.ds(pl.multiple_of(r * 512, 512), 512)
         do_s[rs, :] = nt(dxb_s[rs, :], flat(wo_s[...])).astype(BF)
         return carry
 
-    lax.fori_loop(0, blocks, back_out, 0)
+    lax.fori_loop(0, blocks // 2, back_out, 0)
     store(do_s, do_out)
     o_swap.wait_recv()
     mine = o_st[:, :, :, pl.ds(pl.multiple_of(pc.c * 384, 128), 384)]
@@ -807,10 +804,9 @@
     def pair(j, carry):
         cs = pl.ds(pl.multiple_of(j * 128, 128), 128)
         lane = lane_of(256)
-        above = lax.broadcasted_iota(jnp.int32, (256, 256), 0) <= lax.broadcasted_iota(jnp.int32, (256, 256), 1)
+        col = lax.broadcasted_iota(jnp.int32, (256, 512), 1)
+        above = lax.broadcasted_iota(jnp.int32, (256, 512), 0) <= jnp.where(col >= 256, col - 256, col)
         at = j * 384
-        dk_s[...] = jnp.zeros_like(dk_s)
-        dv_s[...] = jnp.zeros_like(dv_s)
         vaug = jnp.concatenate([v_s[:, cs], ones], axis=1)
         kaug = jnp.concatenate([k_s[:, cs], seg_s[1]], axis=1)
         kt = k_s[:, cs].T
@@ -819,30 +815,32 @@
             rs, first, last = pl.ds(i * 256, 256), i * 256, (i + 1) * 256
             qt, dt = q_s[rs, cs], do_s[rs, cs]
             prod = dt.astype(F32) * o_s[rs, cs].astype(F32)
-            parts = []
+            qms, dms, qas, das = [], [], [], []
             for h in range(2):
                 mask = (lane < 64) == (h == 0)
-                qm, dm = jnp.where(mask, qt, BF(0)), jnp.where(mask, dt, BF(0))
+                qms.append(jnp.where(mask, qt, BF(0)))
+                dms.append(jnp.where(mask, dt, BF(0)))
                 delta = jnp.sum(jnp.where(mask, prod, 0.0), axis=1, keepdims=True)
                 lse = jnp.sum(jnp.where(lane == 2 * j + h, lse_s[rs, :], 0.0), axis=1, keepdims=True)
                 a0, a1, a2 = three_way(-lse)
                 qa = jnp.where(lane == 4, a0, jnp.where(lane == 5, a1, jnp.where(lane == 6, a2, seg_s[0, rs, :])))
                 b0, b1, b2 = three_way(-delta)
                 da = jnp.where(lane == 0, b0, jnp.where(lane == 1, b1, jnp.where(lane == 2, b2, BF(0))))
-                qaug, daug = jnp.concatenate([qm, qa], axis=1), jnp.concatenate([dm, da], axis=1)
-                pd = jnp.exp(jnp.where(above, nt(kaug[first:last], qaug), NEG))
-                dsd = (pd * nt(vaug[first:last], daug)).astype(BF)
-                dv_s[rs, :] += nn(pd.astype(BF), dm)
-                dk_s[rs, :] += nn(dsd, qm)
-                dq = nn(kt[h * 64 : h * 64 + 64, first:last], dsd)
-                if i:
-                    before = pl.ds(0, first)
-                    po = jnp.exp(nt(kaug[:first], qaug))
-                    dso = (po * nt(vaug[:first], daug)).astype(BF)
-                    dv_s[before, :] += nn(po.astype(BF), dm)
-                    dk_s[before, :] += nn(dso, qm)
-                    dq = dq + nn(kt[h * 64 : h * 64 + 64, :first], dso)
-                parts.append(dq)
+                qas.append(jnp.concatenate([qms[h], qa], axis=1))
+                das.append(jnp.concatenate([dms[h], da], axis=1))
+            qm, dm, qaug, daug = (jnp.concatenate(t, axis=0) for t in (qms, dms, qas, das))
+            pd = jnp.exp(jnp.where(above, nt(kaug[first:last], qaug), NEG))
+            dsd = (pd * nt(vaug[first:last], daug)).astype(BF)
+            dv_s[rs, :] = nn(pd.astype(BF), dm)
+            dk_s[rs, :] = nn(dsd, qm)
+            parts = [nn(kt[h * 64 : h * 64 + 64, first:last], dsd[:, h * 256 : h * 256 + 256]) for h in range(2)]
+            if i:
+                before = pl.ds(0, first)
+                po = jnp.exp(nt(kaug[:first], qaug))
+                dso = (po * nt(vaug[:first], daug)).astype(BF)
+                dv_s[before, :] += nn(po.astype(BF), dm)
+                dk_s[before, :] += nn(dso, qm)
+                parts = [parts[h] + nn(kt[h * 64 : h * 64 + 64, :first], dso[:, h * 256 : h * 256 + 256]) for h in range(2)]
             dq = jnp.concatenate(parts, axis=0).T * 0.125
             dq = dq * rope_s[0, rs, :] + turned(dq * rope_s[1, rs, :], lane, True)
             dqkv_s[rs, pl.ds(pl.multiple_of(at, 128), 128)] = dq.astype(BF)
@@ -861,11 +859,11 @@
         ticks.when(j, range(W, W + 6))
 
         def weight(z, carry):
-            rows = nn(h1t_s[pl.ds(pl.multiple_of(z * 192, 64), 192), :], dqkv_s[:, pl.ds(pl.multiple_of(at, 128), 384)])
-            gq_s[j, z] = rows.astype(BF).reshape(4, 48, 384)
+            rows = nn(h1t_s[pl.ds(pl.multiple_of(z * 384, 128), 384), :], dqkv_s[:, pl.ds(pl.multiple_of(at, 128), 384)])
+            gq_s[j, pl.ds(2 * z, 2)] = rows.astype(BF).reshape(2, 4, 48, 384)
             return carry
 
-        lax.fori_loop(0, 4, weight, 0)
+        lax.fori_loop(0, 2, weight, 0)
         for m in range(3):
             pl.when((j // 2 == m) & (lax.rem(j, 2) != pc.c))(q_swaps[m].start)
         return carry
@@ -877,8 +875,9 @@
     gain1 = gain_ref[0:1, :]
 
     def last(r, carry):
-        ticks.when(r, range(L, L + 4))
-        rs = pl.ds(pl.multiple_of(r * 256, 256), 256)
+        for k in range(2):
+            ticks.when(r, range(L + k, L + 4, 2))
+        rs = pl.ds(pl.multiple_of(r * 512, 512), 512)
         dh1 = sum(nt(dqkv_s[rs, m * 768 : (m + 1) * 768], flat(w_s[m])) for m in range(3))
         x = x_s[rs, :].astype(F32)
         r1 = lax.rsqrt(jnp.mean(x * x, axis=1, keepdims=True) + EPS)
@@ -888,7 +887,7 @@
         gx_ref[rs, :] = (dx2_s[rs, :] + r1 * (e1 - n1 * jnp.mean(e1 * n1, axis=1, keepdims=True))).astype(BF)
         return carry
 
-    lax.fori_loop(0, blocks, last, 0)
+    lax.fori_loop(0, blocks // 2, last, 0)
     gg1_s[1:2, 0:768] = gg_ref[0:1, :]
     for w in range(16):
         gg_st[w] = gg1_s[:, 48 * w : 48 * w + 128]

time: 204 us -> 198 us (0.971)
  Pallas kernels: 203 us -> 197 us
    pallas_call x1, Pallas kernels: 82.1 us -> 77.4 us  [fast_body(): hind(q, k, v, o, do, lse, seg, rope, h1t, wqkv, tokens, dx2, gains, gg2,...]
    pallas_call x1, Pallas kernels: 116 us -> 113 us  [fast_body(): fore(seq_lengths, tokens, cotangent, attn_gain[None], ffn_gain[None], w_q...]
where the time goes in v4:
time: 198 us; the launch traced here: 197 us
  Pallas kernels  197 us (99%)
    pallas_call x1, Pallas kernels, fast_body(): fore(seq_lengths, tokens, cotangent, attn_gain[None], ffn_gain[None], w_q...  113 us
    pallas_call x1, Pallas kernels, fast_body(): hind(q, k, v, o, do, lse, seg, rope, h1t, wqkv, tokens, dx2, gains, gg2,...  77.4 us
    pallas_call x1, Pallas kernels, fast_body(): pl.pallas_call(tail_kernel, out_shape=[shape(a.shape, a.dtype) for a in l...  5.68 us

profile of v4, /device:TPU:0, one launch (start us, length us, event | category | flops | bytes accessed | tf_op | source)
XLA Modules:
  0.0 197.4 jit_solution(12637313294332258596)
XLA Ops:
  0.6 113.5 %fore.1 = (bf16[1024,768]{1,0:T(8,128)(2,1)}, bf16[1024,768]{1,0:T(8,128)(2,1)}, bf16[1024,768]{1,0:T(8,128)(2,1)}, bf16[1024,768]{1,0:T(8,128)(2,1)}, bf16[1024...) custom-call(s32[1,4]{1,0:T(1,128)} %lens.1, ...), custom_call_target="tpu_custom_call" | custom-call | tf_op jit(solution)/shard_map/fore/pallas_call | solution.py:963
  114.1 77.4 %hind.1 = (bf16[1024,768]{1,0:T(8,128)(2,1)}, f32[48,768]{1,0:T(8,128)}, f32[48,768]{1,0:T(8,128)}, f32[48,768]{1,0:T(8,128)}, f32[48,768]{1,0:T(8,128)}, /*inde...) custom-call(bf16[1024,768]{1,0:T(8,128)(2,1)} %get-tuple-element.49.q_hbm, ...), custom_call_target="tpu_custom_call" | custom-call | tf_op jit(solution)/shard_map/hind/pallas_call | solution.py:986
  191.6 5.7 %tail.1 = (f32[48,768]{1,0:T(8,128)}, f32[48,768]{1,0:T(8,128)}, f32[48,768]{1,0:T(8,128)}, f32[48,768]{1,0:T(8,128)}, f32[48,2048]{1,0:T(8,128)}, /*index=5*/f3...) custom-call(f32[48,768]{1,0:T(8,128)} %get-tuple-element.66.refs_0_,, ...), custom_call_target="tpu_custom_call" | custom-call | tf_op jit(solution)/shard_map/tail/pallas_call | solution.py:989
